TPU v7x, 32 devices: a whole 2x2x4 slice. The times are simulated.
32 devices in a mesh: lon: 4 (over y, x), lat: 8 (over z, core).
Axes of the slice: x: 2, y: 2, z: 4, core: 2. Of those that a mesh axis runs over, the one named last changes fastest.
Arguments:
- prognostic: bfloat16 [7, 8, 128, 2048], P(None, None, 'lat', 'lon'), may hold values from -6 to 6
- halo_depth: int32 [2, 8, 4], P(None, 'lat', 'lon'), may hold values from 3 to 10, as said below
- cell_offsets: int32 [2, 8, 128, 2048], P(None, None, 'lat', 'lon'), may hold values from -8 to 8, as said below
Outputs:
- advected: bfloat16 [7, 8, 128, 2048], P(None, None, 'lat', 'lon')
Inputs may be any that keep to these rules, and one draw needn't show every extreme that they name: `halo_depth`: every depth is 3 or more; row depths are at most 10, column depths at most 8; some tile has row depth 10 and column depth 8. |cell_offsets[0]| <= (its tile's row depth) - 2 and |cell_offsets[1]| <= (its tile's column depth) - 2; row y + cell_offsets[0] lies in 0 to 126.
All inputs are finite; a program needn't handle non-finite values.
Results may differ from a plain program's by a relative error of at most 0.0047.
Values may be sent and summed in bfloat16 or wider, within the bound.
A program may use at most 64 MiB of HBM per device.

v0:
```python
import math

import jax
import jax.numpy as jnp
from jax import lax
from jax.sharding import PartitionSpec as P

HO = 8
HL = 10
ITERS = 3


courant = 2.0


def passed_along(value, axis, by):
    devices = lax.axis_size(axis)
    pairs = [(i, i + by) for i in range(devices) if 0 <= i + by < devices]
    return lax.ppermute(value, axis, pairs)


def from_behind(value, axis, steps):
    count = lax.axis_size(axis)
    pairs = [(source, (source + steps) % count) for source in range(count)]
    return lax.ppermute(value, axis, pairs)


def keys_kernel(offset):
    magnitude = jnp.abs(offset)
    near_part = (1.5 * magnitude - 2.5) * magnitude * magnitude + 1.0
    far_part = ((-0.5 * magnitude + 2.5) * magnitude - 4.0) * magnitude + 2.0
    return jnp.where(magnitude <= 1.0, near_part, jnp.where(magnitude < 2.0, far_part, 0.0))


def band_sample(extended, row_off, row_frac, col_off, col_frac, row_first, row_span, halo_rows):
    channels = extended.shape[0]
    lat_count, lon_count = row_off.shape
    block_width = min(128, lon_count)
    block_count = lon_count // block_width
    band_width = block_width + 2 * HO
    pieces = lat_count * block_count
    windows = []
    for row_index in range(lat_count):
        for block_index in range(block_count):
            first_col = block_index * block_width
            windows.append(
                extended[
                    :,
                    row_index + row_first : row_index + row_first + row_span,
                    first_col : first_col + band_width,
                ]
            )
    windows = jnp.stack(windows)
    col_start = col_off.reshape(pieces, block_width)
    col_part = col_frac.reshape(pieces, block_width)
    row_start = row_off.reshape(pieces, block_width)
    row_part = row_frac.reshape(pieces, block_width)
    col_rel = (
        jnp.arange(band_width, dtype=jnp.int32)[None, None, :]
        - HO
        - jnp.arange(block_width, dtype=jnp.int32)[None, :, None]
    )
    band_weight = keys_kernel(
        (col_rel - col_start[:, :, None]).astype(jnp.float32) - col_part[:, :, None]
    ).astype(jnp.bfloat16)
    row_rel = jnp.arange(row_span, dtype=jnp.int32)[None, :, None] + (row_first - halo_rows)
    row_weight = keys_kernel(
        (row_rel - row_start[:, None, :]).astype(jnp.float32) - row_part[:, None, :]
    )
    lon_mixed = jnp.einsum(
        "ncrw,niw->ncri", windows, band_weight, preferred_element_type=jnp.float32
    )
    summed = jnp.sum(lon_mixed * row_weight[:, None, :, :], axis=2)
    summed = summed.reshape(lat_count, block_count, channels, block_width)
    return jnp.transpose(summed, (2, 0, 1, 3)).reshape(channels, lat_count, lon_count)


def lat_wrap(fields):
    from_lower = passed_along(fields[:, :, fields.shape[2] - HL :], "lat", 1)
    from_upper = passed_along(fields[:, :, :HL], "lat", -1)
    return jnp.concatenate([from_lower, fields, from_upper], axis=2)


def lon_wrap(fields):
    channels, levels, row_count, col_count = fields.shape
    west_edge = jnp.moveaxis(fields[:, :, :, :HO], 3, 0).reshape(HO, channels * levels * row_count)
    east_edge = jnp.moveaxis(fields[:, :, :, col_count - HO :], 3, 0).reshape(
        HO, channels * levels * row_count
    )
    west_cols = from_behind(east_edge, "lon", 1)
    east_cols = from_behind(west_edge, "lon", -1)
    west_cols = jnp.moveaxis(west_cols.reshape(HO, channels, levels, row_count), 0, 3)
    east_cols = jnp.moveaxis(east_cols.reshape(HO, channels, levels, row_count), 0, 3)
    return jnp.concatenate([west_cols, fields, east_cols], axis=3)


def extend(fields):
    return lon_wrap(lat_wrap(fields))


def on_device(prognostic, halo_depth, cell_offsets):
    channels, levels, lat_count, lon_count = prognostic.shape
    halo_rows = HL
    whole_ext = extend(prognostic)
    wind_ext = whole_ext[0:2]
    lat_total = lat_count * lax.axis_size("lat")
    lat_index = (lax.axis_index("lat") * lat_count + jnp.arange(lat_count, dtype=jnp.int32)).astype(
        jnp.float32
    )
    coslat = jnp.cos((lat_index + 0.5) * (math.pi / lat_total) - 0.5 * math.pi)[:, None]
    rows_depth = halo_depth[0, 0, 0].astype(jnp.float32)
    cols_depth = halo_depth[1, 0, 0].astype(jnp.float32)

    def track_level(level_index):
        wind_level = lax.dynamic_index_in_dim(wind_ext, level_index, 1, keepdims=False)
        offsets_level = lax.dynamic_index_in_dim(cell_offsets, level_index, 1, keepdims=False)
        row_off = offsets_level[0]
        col_off = offsets_level[1]
        row_frac = jnp.full(row_off.shape, 0.5, jnp.float32)
        col_frac = jnp.full(col_off.shape, 0.5, jnp.float32)
        row_mid = jnp.floor_divide(row_off, 2)
        col_mid = jnp.floor_divide(col_off, 2)
        row_float = row_off.astype(jnp.float32)
        col_float = col_off.astype(jnp.float32)
        for repeat in range(ITERS):
            row_part = ((row_off - 2 * row_mid).astype(jnp.float32) + row_frac) * 0.5
            col_part = ((col_off - 2 * col_mid).astype(jnp.float32) + col_frac) * 0.5
            mid_wind = band_sample(
                wind_level,
                row_mid,
                row_part,
                col_mid,
                col_part,
                halo_rows // 2,
                halo_rows + 2,
                halo_rows,
            )
            lon_reach = -courant * mid_wind[0] / coslat
            lat_reach = -courant * mid_wind[1]
            lon_limit = (cols_depth - 1.0) * jnp.tanh(lon_reach / (cols_depth - 1.0))
            lat_limit = (rows_depth - 1.0) * jnp.tanh(lat_reach / (rows_depth - 1.0))
            row_frac = 0.5 + 0.5 * jnp.tanh(0.5 * (lat_limit - row_float - 0.5))
            col_frac = 0.5 + 0.5 * jnp.tanh(0.5 * (lon_limit - col_float - 0.5))
        return (row_frac, col_frac)

    row_fracs, col_fracs = lax.map(track_level, jnp.arange(levels, dtype=jnp.int32))

    def advect_level(level_index):
        fields_level = lax.dynamic_index_in_dim(whole_ext, level_index, 1, keepdims=False)
        offsets_level = lax.dynamic_index_in_dim(cell_offsets, level_index, 1, keepdims=False)
        row_frac = lax.dynamic_index_in_dim(row_fracs, level_index, 0, keepdims=False)
        col_frac = lax.dynamic_index_in_dim(col_fracs, level_index, 0, keepdims=False)
        sampled = band_sample(
            fields_level,
            offsets_level[0],
            row_frac,
            offsets_level[1],
            col_frac,
            1,
            2 * halo_rows,
            halo_rows,
        )
        return sampled.astype(jnp.bfloat16)

    advected = lax.map(advect_level, jnp.arange(levels, dtype=jnp.int32))
    return jnp.moveaxis(advected, 0, 1)


def solution(mesh):
    in_specs = (P(None, None, "lat", "lon"), P(None, "lat", "lon"), P(None, None, "lat", "lon"))
    out_specs = P(None, None, "lat", "lon")
    return jax.shard_map(
        on_device, mesh=mesh, in_specs=in_specs, out_specs=out_specs, check_vma=False
    )
```

profile of v0, /device:TPU:17, one launch (start us, length us, event | category | flops | bytes accessed | tf_op | source)
XLA Modules:
  0.0 350.0 jit_solution(6355525107981728902)
XLA Ops:
  0.0 1.9 fusion.162
  2.3 3.8 %collective-permute-start = (bf16[7,8,10,512]{3,1,2,0:T(8,128)(2,1)S(1)}, bf16[7,8,10,512]{3,1,2,0:T(8,128)(2,1)S(1)}, u32[]{:S(2)}, u32[]{:S(2)}) collective-permute-start(bf16[7,8,10,512]{3,1,2,0:T(8,128)(2,1)S(1)} %copy.79), channel_id=1, source_target_pairs={{0,1},{1,2},{2,3},{3,4},{4,5},{5,6},{6,7},{8,9},{9,10},{10,11},{11... | collective-permute-start | bytes 1720328 | tf_op jit(solution)/shard_map/ppermute | solution.py:19
  6.4 1.9 collective-permute-start.1
  8.3 4.4 %collective-permute-done = bf16[7,8,10,512]{3,1,2,0:T(8,128)(2,1)S(1)} collective-permute-done((bf16[7,8,10,512]{3,1,2,0:T(8,128)(2,1)S(1)}, bf16[7,8,10,512]{3,1,2,0:T(8,128)(2,1)S(1)}, u32[]{:S(2)}, u32[]{:S(2)}) %collective-permute-start) | collective-permute-done | bytes 573472 | tf_op jit(solution)/shard_map/ppermute | solution.py:19
  12.9 4.5 %collective-permute-done.1 = bf16[7,8,10,512]{3,1,2,0:T(8,128)(2,1)S(1)} collective-permute-done((bf16[7,8,10,512]{3,1,2,0:T(8,128)(2,1)S(1)}, bf16[7,8,10,512]{3,1,2,0:T(8,128)(2,1)S(1)}, u32[]{:S(2)}, u32[]{:S(2)}) %collective-permute-start.1) | collective-permute-done | bytes 573472 | tf_op jit(solution)/shard_map/ppermute | solution.py:19
  28.5 5.3 %pad_maximum_fusion = bf16[7,8,36,528]{3,2,0,1:T(8,128)(2,1)} fusion(bf16[7,8,36,8]{3,2,0,1:T(8,128)(2,1)} %copy.59, bf16[7,8,10,512]{3,2,0,1:T(8,128)(2,1)S(1)} %copy.55, bf16[7,8,10,512]{3,2,0,1:T(8,128)(2,1)S(1)} %copy.53, bf16[7,8,36,8]{3,2,0,1:T(8,128)(2,1)S(1)} %copy.58, bf16[7,8,16,512]{3,2,1,0:T(8,128)(2,1)S(1)} %copy-done), kind=kLoop, calls=%fused_computation.464 | loop fusion | flops 10644480 | bytes 4257792 | tf_op jit(solution)/shard_map/concatenate | solution.py:94
  35.0 168.7 %while.30 = (s32[]{:T(128)}, f32[8,16,512]{2,0,1:T(8,128)}, f32[8,16,512]{2,0,1:T(8,128)}, f32[]{:T(128)}, s32[8]{0:T(128)S(1)}, /*index=5*/bf16[2,8,36,528]{3,2...) while((s32[]{:T(128)}, f32[8,16,512]{2,0,1:T(8,128)}, ...), condition=%wide.region_4.5_spmd.clone, body=%wide.region_0.4_spmd.clone.sunk | while | flops 249071872 | bytes 9238763 | solution.py:146
  39.8 3.6 %fusion.198 = f32[64,2,128]{2,1,0:T(2,128)S(1)} fusion(bf16[64,2,12,144]{3,2,1,0:T(8,128)(2,1)S(1)} %constant_dynamic-update-slice_fusion.383, f32[64,128]{1,0:T(8,128)S(1)} %add_multiply_fusion.12, s32[64,128]{1,0:T(8,128)S(1)} %add_select_fusion.4, s32[128,144]{0,1:T(8,128)S(1)} %iota_subtract_fusion.5, f32[64,12,128]{2,1,0:T(8,128)S(1)} %fusion.197), kind=kOutput, calls=%fused_computation.235.clone.1 | convolution fusion | flops 80592896 | bytes 1040384 | tf_op jit(solution)/shard_map/while/body/eval_jaxpr/ncrw,niw->ncri/dot_general | solution.py:70
  44.3 3.6 %fusion.202 = f32[64,2,128]{2,1,0:T(2,128)S(1)} fusion(bf16[64,2,12,144]{3,2,1,0:T(8,128)(2,1)S(1)} %constant_dynamic-update-slice_fusion.383, f32[64,128]{1,0:T(8,128)S(1)} %add_multiply_fusion.14, s32[64,128]{1,0:T(8,128)S(1)} %add_select_fusion.4, s32[128,144]{0,1:T(8,128)S(1)} %iota_subtract_fusion.5, f32[64,12,128]{2,1,0:T(8,128)S(1)} %fusion.201), kind=kOutput, calls=%fused_computation.236.clone.1 | convolution fusion | flops 80592896 | bytes 1040384 | tf_op jit(solution)/shard_map/while/body/eval_jaxpr/ncrw,niw->ncri/dot_general | solution.py:70
  48.6 3.6 %fusion.205 = f32[64,2,128]{2,1,0:T(2,128)S(1)} fusion(bf16[64,2,12,144]{3,2,1,0:T(8,128)(2,1)S(1)} %constant_dynamic-update-slice_fusion.383, f32[64,128]{1,0:T(8,128)S(1)} %add_multiply_fusion.16, s32[64,128]{1,0:T(8,128)S(1)} %add_select_fusion.4, s32[128,144]{0,1:T(8,128)S(1)} %iota_subtract_fusion.5, f32[64,12,128]{2,1,0:T(8,128)S(1)} %fusion.204), kind=kOutput, calls=%fused_computation.237.clone.1 | convolution fusion | flops 80592896 | bytes 1040384 | tf_op jit(solution)/shard_map/while/body/eval_jaxpr/ncrw,niw->ncri/dot_general | solution.py:70
  52.6 1.8 dynamic_update_slice.31
  54.3 1.8 dynamic_update_slice.30
  60.9 3.6 %fusion.198 = f32[64,2,128]{2,1,0:T(2,128)S(1)} fusion(bf16[64,2,12,144]{3,2,1,0:T(8,128)(2,1)S(1)} %constant_dynamic-update-slice_fusion.383, f32[64,128]{1,0:T(8,128)S(1)} %add_multiply_fusion.12, s32[64,128]{1,0:T(8,128)S(1)} %add_select_fusion.4, s32[128,144]{0,1:T(8,128)S(1)} %iota_subtract_fusion.5, f32[64,12,128]{2,1,0:T(8,128)S(1)} %fusion.197), kind=kOutput, calls=%fused_computation.235.clone.1 | convolution fusion | flops 80592896 | bytes 1040384 | tf_op jit(solution)/shard_map/while/body/eval_jaxpr/ncrw,niw->ncri/dot_general | solution.py:70
  65.4 3.6 %fusion.202 = f32[64,2,128]{2,1,0:T(2,128)S(1)} fusion(bf16[64,2,12,144]{3,2,1,0:T(8,128)(2,1)S(1)} %constant_dynamic-update-slice_fusion.383, f32[64,128]{1,0:T(8,128)S(1)} %add_multiply_fusion.14, s32[64,128]{1,0:T(8,128)S(1)} %add_select_fusion.4, s32[128,144]{0,1:T(8,128)S(1)} %iota_subtract_fusion.5, f32[64,12,128]{2,1,0:T(8,128)S(1)} %fusion.201), kind=kOutput, calls=%fused_computation.236.clone.1 | convolution fusion | flops 80592896 | bytes 1040384 | tf_op jit(solution)/shard_map/while/body/eval_jaxpr/ncrw,niw->ncri/dot_general | solution.py:70
  69.7 3.6 %fusion.205 = f32[64,2,128]{2,1,0:T(2,128)S(1)} fusion(bf16[64,2,12,144]{3,2,1,0:T(8,128)(2,1)S(1)} %constant_dynamic-update-slice_fusion.383, f32[64,128]{1,0:T(8,128)S(1)} %add_multiply_fusion.16, s32[64,128]{1,0:T(8,128)S(1)} %add_select_fusion.4, s32[128,144]{0,1:T(8,128)S(1)} %iota_subtract_fusion.5, f32[64,12,128]{2,1,0:T(8,128)S(1)} %fusion.204), kind=kOutput, calls=%fused_computation.237.clone.1 | convolution fusion | flops 80592896 | bytes 1040384 | tf_op jit(solution)/shard_map/while/body/eval_jaxpr/ncrw,niw->ncri/dot_general | solution.py:70
  73.6 1.8 dynamic_update_slice.31
  75.4 1.8 dynamic_update_slice.30
  82.0 3.6 %fusion.198 = f32[64,2,128]{2,1,0:T(2,128)S(1)} fusion(bf16[64,2,12,144]{3,2,1,0:T(8,128)(2,1)S(1)} %constant_dynamic-update-slice_fusion.383, f32[64,128]{1,0:T(8,128)S(1)} %add_multiply_fusion.12, s32[64,128]{1,0:T(8,128)S(1)} %add_select_fusion.4, s32[128,144]{0,1:T(8,128)S(1)} %iota_subtract_fusion.5, f32[64,12,128]{2,1,0:T(8,128)S(1)} %fusion.197), kind=kOutput, calls=%fused_computation.235.clone.1 | convolution fusion | flops 80592896 | bytes 1040384 | tf_op jit(solution)/shard_map/while/body/eval_jaxpr/ncrw,niw->ncri/dot_general | solution.py:70
  86.5 3.6 %fusion.202 = f32[64,2,128]{2,1,0:T(2,128)S(1)} fusion(bf16[64,2,12,144]{3,2,1,0:T(8,128)(2,1)S(1)} %constant_dynamic-update-slice_fusion.383, f32[64,128]{1,0:T(8,128)S(1)} %add_multiply_fusion.14, s32[64,128]{1,0:T(8,128)S(1)} %add_select_fusion.4, s32[128,144]{0,1:T(8,128)S(1)} %iota_subtract_fusion.5, f32[64,12,128]{2,1,0:T(8,128)S(1)} %fusion.201), kind=kOutput, calls=%fused_computation.236.clone.1 | convolution fusion | flops 80592896 | bytes 1040384 | tf_op jit(solution)/shard_map/while/body/eval_jaxpr/ncrw,niw->ncri/dot_general | solution.py:70
  90.8 3.6 %fusion.205 = f32[64,2,128]{2,1,0:T(2,128)S(1)} fusion(bf16[64,2,12,144]{3,2,1,0:T(8,128)(2,1)S(1)} %constant_dynamic-update-slice_fusion.383, f32[64,128]{1,0:T(8,128)S(1)} %add_multiply_fusion.16, s32[64,128]{1,0:T(8,128)S(1)} %add_select_fusion.4, s32[128,144]{0,1:T(8,128)S(1)} %iota_subtract_fusion.5, f32[64,12,128]{2,1,0:T(8,128)S(1)} %fusion.204), kind=kOutput, calls=%fused_computation.237.clone.1 | convolution fusion | flops 80592896 | bytes 1040384 | tf_op jit(solution)/shard_map/while/body/eval_jaxpr/ncrw,niw->ncri/dot_general | solution.py:70
  94.7 1.8 dynamic_update_slice.31
  96.5 1.8 dynamic_update_slice.30
  103.1 3.6 %fusion.198 = f32[64,2,128]{2,1,0:T(2,128)S(1)} fusion(bf16[64,2,12,144]{3,2,1,0:T(8,128)(2,1)S(1)} %constant_dynamic-update-slice_fusion.383, f32[64,128]{1,0:T(8,128)S(1)} %add_multiply_fusion.12, s32[64,128]{1,0:T(8,128)S(1)} %add_select_fusion.4, s32[128,144]{0,1:T(8,128)S(1)} %iota_subtract_fusion.5, f32[64,12,128]{2,1,0:T(8,128)S(1)} %fusion.197), kind=kOutput, calls=%fused_computation.235.clone.1 | convolution fusion | flops 80592896 | bytes 1040384 | tf_op jit(solution)/shard_map/while/body/eval_jaxpr/ncrw,niw->ncri/dot_general | solution.py:70
  107.6 3.6 %fusion.202 = f32[64,2,128]{2,1,0:T(2,128)S(1)} fusion(bf16[64,2,12,144]{3,2,1,0:T(8,128)(2,1)S(1)} %constant_dynamic-update-slice_fusion.383, f32[64,128]{1,0:T(8,128)S(1)} %add_multiply_fusion.14, s32[64,128]{1,0:T(8,128)S(1)} %add_select_fusion.4, s32[128,144]{0,1:T(8,128)S(1)} %iota_subtract_fusion.5, f32[64,12,128]{2,1,0:T(8,128)S(1)} %fusion.201), kind=kOutput, calls=%fused_computation.236.clone.1 | convolution fusion | flops 80592896 | bytes 1040384 | tf_op jit(solution)/shard_map/while/body/eval_jaxpr/ncrw,niw->ncri/dot_general | solution.py:70
  111.9 3.6 %fusion.205 = f32[64,2,128]{2,1,0:T(2,128)S(1)} fusion(bf16[64,2,12,144]{3,2,1,0:T(8,128)(2,1)S(1)} %constant_dynamic-update-slice_fusion.383, f32[64,128]{1,0:T(8,128)S(1)} %add_multiply_fusion.16, s32[64,128]{1,0:T(8,128)S(1)} %add_select_fusion.4, s32[128,144]{0,1:T(8,128)S(1)} %iota_subtract_fusion.5, f32[64,12,128]{2,1,0:T(8,128)S(1)} %fusion.204), kind=kOutput, calls=%fused_computation.237.clone.1 | convolution fusion | flops 80592896 | bytes 1040384 | tf_op jit(solution)/shard_map/while/body/eval_jaxpr/ncrw,niw->ncri/dot_general | solution.py:70
  115.8 1.8 dynamic_update_slice.31
  117.6 1.8 dynamic_update_slice.30
  124.2 3.6 %fusion.198 = f32[64,2,128]{2,1,0:T(2,128)S(1)} fusion(bf16[64,2,12,144]{3,2,1,0:T(8,128)(2,1)S(1)} %constant_dynamic-update-slice_fusion.383, f32[64,128]{1,0:T(8,128)S(1)} %add_multiply_fusion.12, s32[64,128]{1,0:T(8,128)S(1)} %add_select_fusion.4, s32[128,144]{0,1:T(8,128)S(1)} %iota_subtract_fusion.5, f32[64,12,128]{2,1,0:T(8,128)S(1)} %fusion.197), kind=kOutput, calls=%fused_computation.235.clone.1 | convolution fusion | flops 80592896 | bytes 1040384 | tf_op jit(solution)/shard_map/while/body/eval_jaxpr/ncrw,niw->ncri/dot_general | solution.py:70
  128.7 3.6 %fusion.202 = f32[64,2,128]{2,1,0:T(2,128)S(1)} fusion(bf16[64,2,12,144]{3,2,1,0:T(8,128)(2,1)S(1)} %constant_dynamic-update-slice_fusion.383, f32[64,128]{1,0:T(8,128)S(1)} %add_multiply_fusion.14, s32[64,128]{1,0:T(8,128)S(1)} %add_select_fusion.4, s32[128,144]{0,1:T(8,128)S(1)} %iota_subtract_fusion.5, f32[64,12,128]{2,1,0:T(8,128)S(1)} %fusion.201), kind=kOutput, calls=%fused_computation.236.clone.1 | convolution fusion | flops 80592896 | bytes 1040384 | tf_op jit(solution)/shard_map/while/body/eval_jaxpr/ncrw,niw->ncri/dot_general | solution.py:70
  133.0 3.6 %fusion.205 = f32[64,2,128]{2,1,0:T(2,128)S(1)} fusion(bf16[64,2,12,144]{3,2,1,0:T(8,128)(2,1)S(1)} %constant_dynamic-update-slice_fusion.383, f32[64,128]{1,0:T(8,128)S(1)} %add_multiply_fusion.16, s32[64,128]{1,0:T(8,128)S(1)} %add_select_fusion.4, s32[128,144]{0,1:T(8,128)S(1)} %iota_subtract_fusion.5, f32[64,12,128]{2,1,0:T(8,128)S(1)} %fusion.204), kind=kOutput, calls=%fused_computation.237.clone.1 | convolution fusion | flops 80592896 | bytes 1040384 | tf_op jit(solution)/shard_map/while/body/eval_jaxpr/ncrw,niw->ncri/dot_general | solution.py:70
  136.9 1.8 dynamic_update_slice.31
  138.7 1.8 dynamic_update_slice.30
  145.3 3.6 %fusion.198 = f32[64,2,128]{2,1,0:T(2,128)S(1)} fusion(bf16[64,2,12,144]{3,2,1,0:T(8,128)(2,1)S(1)} %constant_dynamic-update-slice_fusion.383, f32[64,128]{1,0:T(8,128)S(1)} %add_multiply_fusion.12, s32[64,128]{1,0:T(8,128)S(1)} %add_select_fusion.4, s32[128,144]{0,1:T(8,128)S(1)} %iota_subtract_fusion.5, f32[64,12,128]{2,1,0:T(8,128)S(1)} %fusion.197), kind=kOutput, calls=%fused_computation.235.clone.1 | convolution fusion | flops 80592896 | bytes 1040384 | tf_op jit(solution)/shard_map/while/body/eval_jaxpr/ncrw,niw->ncri/dot_general | solution.py:70
  149.8 3.6 %fusion.202 = f32[64,2,128]{2,1,0:T(2,128)S(1)} fusion(bf16[64,2,12,144]{3,2,1,0:T(8,128)(2,1)S(1)} %constant_dynamic-update-slice_fusion.383, f32[64,128]{1,0:T(8,128)S(1)} %add_multiply_fusion.14, s32[64,128]{1,0:T(8,128)S(1)} %add_select_fusion.4, s32[128,144]{0,1:T(8,128)S(1)} %iota_subtract_fusion.5, f32[64,12,128]{2,1,0:T(8,128)S(1)} %fusion.201), kind=kOutput, calls=%fused_computation.236.clone.1 | convolution fusion | flops 80592896 | bytes 1040384 | tf_op jit(solution)/shard_map/while/body/eval_jaxpr/ncrw,niw->ncri/dot_general | solution.py:70
  154.0 3.6 %fusion.205 = f32[64,2,128]{2,1,0:T(2,128)S(1)} fusion(bf16[64,2,12,144]{3,2,1,0:T(8,128)(2,1)S(1)} %constant_dynamic-update-slice_fusion.383, f32[64,128]{1,0:T(8,128)S(1)} %add_multiply_fusion.16, s32[64,128]{1,0:T(8,128)S(1)} %add_select_fusion.4, s32[128,144]{0,1:T(8,128)S(1)} %iota_subtract_fusion.5, f32[64,12,128]{2,1,0:T(8,128)S(1)} %fusion.204), kind=kOutput, calls=%fused_computation.237.clone.1 | convolution fusion | flops 80592896 | bytes 1040384 | tf_op jit(solution)/shard_map/while/body/eval_jaxpr/ncrw,niw->ncri/dot_general | solution.py:70
  158.0 1.8 dynamic_update_slice.31
  159.8 1.8 dynamic_update_slice.30
  166.4 3.6 %fusion.198 = f32[64,2,128]{2,1,0:T(2,128)S(1)} fusion(bf16[64,2,12,144]{3,2,1,0:T(8,128)(2,1)S(1)} %constant_dynamic-update-slice_fusion.383, f32[64,128]{1,0:T(8,128)S(1)} %add_multiply_fusion.12, s32[64,128]{1,0:T(8,128)S(1)} %add_select_fusion.4, s32[128,144]{0,1:T(8,128)S(1)} %iota_subtract_fusion.5, f32[64,12,128]{2,1,0:T(8,128)S(1)} %fusion.197), kind=kOutput, calls=%fused_computation.235.clone.1 | convolution fusion | flops 80592896 | bytes 1040384 | tf_op jit(solution)/shard_map/while/body/eval_jaxpr/ncrw,niw->ncri/dot_general | solution.py:70
  170.9 3.6 %fusion.202 = f32[64,2,128]{2,1,0:T(2,128)S(1)} fusion(bf16[64,2,12,144]{3,2,1,0:T(8,128)(2,1)S(1)} %constant_dynamic-update-slice_fusion.383, f32[64,128]{1,0:T(8,128)S(1)} %add_multiply_fusion.14, s32[64,128]{1,0:T(8,128)S(1)} %add_select_fusion.4, s32[128,144]{0,1:T(8,128)S(1)} %iota_subtract_fusion.5, f32[64,12,128]{2,1,0:T(8,128)S(1)} %fusion.201), kind=kOutput, calls=%fused_computation.236.clone.1 | convolution fusion | flops 80592896 | bytes 1040384 | tf_op jit(solution)/shard_map/while/body/eval_jaxpr/ncrw,niw->ncri/dot_general | solution.py:70
  175.1 3.6 %fusion.205 = f32[64,2,128]{2,1,0:T(2,128)S(1)} fusion(bf16[64,2,12,144]{3,2,1,0:T(8,128)(2,1)S(1)} %constant_dynamic-update-slice_fusion.383, f32[64,128]{1,0:T(8,128)S(1)} %add_multiply_fusion.16, s32[64,128]{1,0:T(8,128)S(1)} %add_select_fusion.4, s32[128,144]{0,1:T(8,128)S(1)} %iota_subtract_fusion.5, f32[64,12,128]{2,1,0:T(8,128)S(1)} %fusion.204), kind=kOutput, calls=%fused_computation.237.clone.1 | convolution fusion | flops 80592896 | bytes 1040384 | tf_op jit(solution)/shard_map/while/body/eval_jaxpr/ncrw,niw->ncri/dot_general | solution.py:70
  179.1 1.8 dynamic_update_slice.31
  180.8 1.8 dynamic_update_slice.30
  187.4 3.6 %fusion.198 = f32[64,2,128]{2,1,0:T(2,128)S(1)} fusion(bf16[64,2,12,144]{3,2,1,0:T(8,128)(2,1)S(1)} %constant_dynamic-update-slice_fusion.383, f32[64,128]{1,0:T(8,128)S(1)} %add_multiply_fusion.12, s32[64,128]{1,0:T(8,128)S(1)} %add_select_fusion.4, s32[128,144]{0,1:T(8,128)S(1)} %iota_subtract_fusion.5, f32[64,12,128]{2,1,0:T(8,128)S(1)} %fusion.197), kind=kOutput, calls=%fused_computation.235.clone.1 | convolution fusion | flops 80592896 | bytes 1040384 | tf_op jit(solution)/shard_map/while/body/eval_jaxpr/ncrw,niw->ncri/dot_general | solution.py:70
  191.9 3.6 %fusion.202 = f32[64,2,128]{2,1,0:T(2,128)S(1)} fusion(bf16[64,2,12,144]{3,2,1,0:T(8,128)(2,1)S(1)} %constant_dynamic-update-slice_fusion.383, f32[64,128]{1,0:T(8,128)S(1)} %add_multiply_fusion.14, s32[64,128]{1,0:T(8,128)S(1)} %add_select_fusion.4, s32[128,144]{0,1:T(8,128)S(1)} %iota_subtract_fusion.5, f32[64,12,128]{2,1,0:T(8,128)S(1)} %fusion.201), kind=kOutput, calls=%fused_computation.236.clone.1 | convolution fusion | flops 80592896 | bytes 1040384 | tf_op jit(solution)/shard_map/while/body/eval_jaxpr/ncrw,niw->ncri/dot_general | solution.py:70
  196.2 3.6 %fusion.205 = f32[64,2,128]{2,1,0:T(2,128)S(1)} fusion(bf16[64,2,12,144]{3,2,1,0:T(8,128)(2,1)S(1)} %constant_dynamic-update-slice_fusion.383, f32[64,128]{1,0:T(8,128)S(1)} %add_multiply_fusion.16, s32[64,128]{1,0:T(8,128)S(1)} %add_select_fusion.4, s32[128,144]{0,1:T(8,128)S(1)} %iota_subtract_fusion.5, f32[64,12,128]{2,1,0:T(8,128)S(1)} %fusion.204), kind=kOutput, calls=%fused_computation.237.clone.1 | convolution fusion | flops 80592896 | bytes 1040384 | tf_op jit(solution)/shard_map/while/body/eval_jaxpr/ncrw,niw->ncri/dot_general | solution.py:70
  200.2 1.8 dynamic_update_slice.31
  201.9 1.8 dynamic_update_slice.30
  203.7 146.3 %while.29 = (s32[]{:T(128)}, bf16[8,7,16,512]{3,2,0,1:T(8,128)(2,1)}, s32[8]{0:T(128)S(1)}, bf16[7,8,36,528]{3,2,0,1:T(8,128)(2,1)}, s32[2,8,16,512]{3,2,1,0:T(8...) while((s32[]{:T(128)}, ...), condition=%wide.region_7.8_spmd, body=%wide.region_5.7_spmd.sunk | while | flops 359262368 | bytes 27186292 | solution.py:165
  209.0 2.4 copy-done.1
  214.0 7.2 %multiply_reduce_fusion.2 = bf16[64,7,128]{2,1,0:T(8,128)(2,1)S(1)} fusion(f32[64,20,128]{2,1,0:T(8,128)S(1)} %fusion.190, bf16[64,7,20,144]{3,2,1,0:T(8,128)(2,1)} %copy-done.1, f32[64,128]{1,0:T(8,128)S(1)} %bitcast.958, s32[64,128]{1,0:T(8,128)S(1)} %sub.1205, s32[128,144]{0,1:T(8,128)S(1)} %iota_subtract_fusion.4), kind=kOutput, calls=%fused_computation.2.clone.1 | convolution fusion | flops 356130816 | bytes 3489792 | tf_op jit(solution)/shard_map/while/body/eval_jaxpr/ncrw,niw->ncri/dot_general | solution.py:70
  227.3 2.4 copy-done.1
  232.2 7.2 %multiply_reduce_fusion.2 = bf16[64,7,128]{2,1,0:T(8,128)(2,1)S(1)} fusion(f32[64,20,128]{2,1,0:T(8,128)S(1)} %fusion.190, bf16[64,7,20,144]{3,2,1,0:T(8,128)(2,1)} %copy-done.1, f32[64,128]{1,0:T(8,128)S(1)} %bitcast.958, s32[64,128]{1,0:T(8,128)S(1)} %sub.1205, s32[128,144]{0,1:T(8,128)S(1)} %iota_subtract_fusion.4), kind=kOutput, calls=%fused_computation.2.clone.1 | convolution fusion | flops 356130816 | bytes 3489792 | tf_op jit(solution)/shard_map/while/body/eval_jaxpr/ncrw,niw->ncri/dot_general | solution.py:70
  245.6 2.4 copy-done.1
  250.5 7.2 %multiply_reduce_fusion.2 = bf16[64,7,128]{2,1,0:T(8,128)(2,1)S(1)} fusion(f32[64,20,128]{2,1,0:T(8,128)S(1)} %fusion.190, bf16[64,7,20,144]{3,2,1,0:T(8,128)(2,1)} %copy-done.1, f32[64,128]{1,0:T(8,128)S(1)} %bitcast.958, s32[64,128]{1,0:T(8,128)S(1)} %sub.1205, s32[128,144]{0,1:T(8,128)S(1)} %iota_subtract_fusion.4), kind=kOutput, calls=%fused_computation.2.clone.1 | convolution fusion | flops 356130816 | bytes 3489792 | tf_op jit(solution)/shard_map/while/body/eval_jaxpr/ncrw,niw->ncri/dot_general | solution.py:70
  263.9 2.4 copy-done.1
  268.8 7.2 %multiply_reduce_fusion.2 = bf16[64,7,128]{2,1,0:T(8,128)(2,1)S(1)} fusion(f32[64,20,128]{2,1,0:T(8,128)S(1)} %fusion.190, bf16[64,7,20,144]{3,2,1,0:T(8,128)(2,1)} %copy-done.1, f32[64,128]{1,0:T(8,128)S(1)} %bitcast.958, s32[64,128]{1,0:T(8,128)S(1)} %sub.1205, s32[128,144]{0,1:T(8,128)S(1)} %iota_subtract_fusion.4), kind=kOutput, calls=%fused_computation.2.clone.1 | convolution fusion | flops 356130816 | bytes 3489792 | tf_op jit(solution)/shard_map/while/body/eval_jaxpr/ncrw,niw->ncri/dot_general | solution.py:70
  282.1 2.4 copy-done.1
  287.1 7.2 %multiply_reduce_fusion.2 = bf16[64,7,128]{2,1,0:T(8,128)(2,1)S(1)} fusion(f32[64,20,128]{2,1,0:T(8,128)S(1)} %fusion.190, bf16[64,7,20,144]{3,2,1,0:T(8,128)(2,1)} %copy-done.1, f32[64,128]{1,0:T(8,128)S(1)} %bitcast.958, s32[64,128]{1,0:T(8,128)S(1)} %sub.1205, s32[128,144]{0,1:T(8,128)S(1)} %iota_subtract_fusion.4), kind=kOutput, calls=%fused_computation.2.clone.1 | convolution fusion | flops 356130816 | bytes 3489792 | tf_op jit(solution)/shard_map/while/body/eval_jaxpr/ncrw,niw->ncri/dot_general | solution.py:70
  300.4 2.4 copy-done.1
  305.4 7.2 %multiply_reduce_fusion.2 = bf16[64,7,128]{2,1,0:T(8,128)(2,1)S(1)} fusion(f32[64,20,128]{2,1,0:T(8,128)S(1)} %fusion.190, bf16[64,7,20,144]{3,2,1,0:T(8,128)(2,1)} %copy-done.1, f32[64,128]{1,0:T(8,128)S(1)} %bitcast.958, s32[64,128]{1,0:T(8,128)S(1)} %sub.1205, s32[128,144]{0,1:T(8,128)S(1)} %iota_subtract_fusion.4), kind=kOutput, calls=%fused_computation.2.clone.1 | convolution fusion | flops 356130816 | bytes 3489792 | tf_op jit(solution)/shard_map/while/body/eval_jaxpr/ncrw,niw->ncri/dot_general | solution.py:70
  318.7 2.4 copy-done.1
  323.7 7.2 %multiply_reduce_fusion.2 = bf16[64,7,128]{2,1,0:T(8,128)(2,1)S(1)} fusion(f32[64,20,128]{2,1,0:T(8,128)S(1)} %fusion.190, bf16[64,7,20,144]{3,2,1,0:T(8,128)(2,1)} %copy-done.1, f32[64,128]{1,0:T(8,128)S(1)} %bitcast.958, s32[64,128]{1,0:T(8,128)S(1)} %sub.1205, s32[128,144]{0,1:T(8,128)S(1)} %iota_subtract_fusion.4), kind=kOutput, calls=%fused_computation.2.clone.1 | convolution fusion | flops 356130816 | bytes 3489792 | tf_op jit(solution)/shard_map/while/body/eval_jaxpr/ncrw,niw->ncri/dot_general | solution.py:70
  337.0 2.4 copy-done.1
  341.9 7.2 %multiply_reduce_fusion.2 = bf16[64,7,128]{2,1,0:T(8,128)(2,1)S(1)} fusion(f32[64,20,128]{2,1,0:T(8,128)S(1)} %fusion.190, bf16[64,7,20,144]{3,2,1,0:T(8,128)(2,1)} %copy-done.1, f32[64,128]{1,0:T(8,128)S(1)} %bitcast.958, s32[64,128]{1,0:T(8,128)S(1)} %sub.1205, s32[128,144]{0,1:T(8,128)S(1)} %iota_subtract_fusion.4), kind=kOutput, calls=%fused_computation.2.clone.1 | convolution fusion | flops 356130816 | bytes 3489792 | tf_op jit(solution)/shard_map/while/body/eval_jaxpr/ncrw,niw->ncri/dot_general | solution.py:70
  (1444 shorter events, 97.5 us)
Async XLA Ops:
  0.0 17.6 %copy-start = (bf16[7,8,16,512]{3,2,1,0:T(8,128)(2,1)S(1)}, bf16[7,8,16,512]{3,2,1,0:T(8,128)(2,1)}, u32[]{:S(2)}) copy-start(bf16[7,8,16,512]{3,2,1,0:T(8,128)(2,1)} %param.7) | copy-start | bytes 2752516
  1.9 21.8 %copy-start.2 = (s32[2,1,1]{0,2,1:T(1,128)S(1)}, s32[2,1,1]{0,2,1:T(1,128)}, u32[]{:S(2)}) copy-start(s32[2,1,1]{0,2,1:T(1,128)} %param.8) | copy-start | bytes 28
  2.3 10.4 %collective-permute-start = (bf16[7,8,10,512]{3,1,2,0:T(8,128)(2,1)S(1)}, bf16[7,8,10,512]{3,1,2,0:T(8,128)(2,1)S(1)}, u32[]{:S(2)}, u32[]{:S(2)}) collective-permute-start(bf16[7,8,10,512]{3,1,2,0:T(8,128)(2,1)S(1)} %copy.79), channel_id=1, source_target_pairs={{0,1},{1,2},{2,3},{3,4},{4,5},{5,6},{6,7},{8,9},{9,10},{10,11},{11... | collective-permute-start | bytes 1720328 | tf_op jit(solution)/shard_map/ppermute | solution.py:19
  6.4 11.0 %collective-permute-start.1 = (bf16[7,8,10,512]{3,1,2,0:T(8,128)(2,1)S(1)}, bf16[7,8,10,512]{3,1,2,0:T(8,128)(2,1)S(1)}, u32[]{:S(2)}, u32[]{:S(2)}) collective-permute-start(bf16[7,8,10,512]{3,1,2,0:T(8,128)(2,1)S(1)} %copy.80), channel_id=1, source_target_pairs={{1,0},{2,1},{3,2},{4,3},{5,4},{6,5},{7,6},{9,8},{10,9},{11,10},{12... | collective-permute-start | bytes 1720328 | tf_op jit(solution)/shard_map/ppermute | solution.py:19
  20.5 5.1 %collective-permute-start.2 = (bf16[8,2016]{1,0:T(8,128)(2,1)S(1)}, bf16[8,2016]{1,0:T(8,128)(2,1)S(1)}, u32[]{:S(2)}, u32[]{:S(2)}) collective-permute-start(bf16[8,2016]{1,0:T(8,128)(2,1)S(1)} %reshape.788), channel_id=1, source_target_pairs={{0,8},{8,16},{16,24},{24,0},{1,9},{9,17},{17,25},{25,1},{2,10},{10... | collective-permute-start | bytes 96776 | tf_op jit(solution)/shard_map/ppermute | solution.py:25
  22.3 3.9 %collective-permute-start.3 = (bf16[8,2016]{1,0:T(8,128)(2,1)S(1)}, bf16[8,2016]{1,0:T(8,128)(2,1)}, u32[]{:S(2)}, u32[]{:S(2)}) collective-permute-start(bf16[8,2016]{1,0:T(8,128)(2,1)S(1)} %reshape.790), channel_id=1, source_target_pairs={{0,24},{8,0},{16,8},{24,16},{1,25},{9,1},{17,9},{25,17},{2,26},{10... | collective-permute-start | bytes 96776 | tf_op jit(solution)/shard_map/ppermute | solution.py:25
  209.0 2.4 copy-start.1
  227.3 2.4 copy-start.1
  245.6 2.4 copy-start.1
  263.9 2.4 copy-start.1
  282.1 2.4 copy-start.1
  300.4 2.4 copy-start.1
  318.7 2.4 copy-start.1
  337.0 2.4 copy-start.1
where the time goes:
time: 354 us; the launch traced here: 350 us
  matrix products  145 us (41%)
  local copies, waits for them, and re-layouts  122 us (34%)
  loops' own time  37.2 us (11%)
  other arithmetic  27.8 us (8%)
  waiting for transfers between devices  8.88 us (3%)
  starting transfers between devices  8.34 us (2%)
    dot_general x32, matrix products, band_sample(): jnp.einsum('ncrw,niw->ncri', windows, band_weight, preferred_element_type...  145 us
    while x1040, local copies, waits for them, and re-layouts  36.1 us
    dynamic_update_slice x16, local copies, waits for them, and re-layouts, on_device(): lax.map(track_level, jnp.arange(levels, dtype=jnp.int32))  28.3 us
    another operation x1, loops' own time, on_device(): lax.map(track_level, jnp.arange(levels, dtype=jnp.int32))  19.1 us
    another operation x1, loops' own time, on_device(): advected = lax.map(advect_level, jnp.arange(levels, dtype=jnp.int32))  18.1 us
    select_n x32, other arithmetic, keys_kernel(): jnp.where(magnitude <= 1.0, near_part, jnp.where(magnitude < 2.0, far_par...  13.9 us
    dynamic_slice x16, local copies, waits for them, and re-layouts, on_device(): lax.map(track_level, jnp.arange(levels, dtype=jnp.int32))  9.21 us
    ppermute x2, waiting for transfers between devices, passed_along(): return lax.ppermute(value, axis, pairs)  8.88 us
  transfers between devices with their start and end apart: 4, of which 2 were waited for; matrix products, arithmetic and copies ran while one was open for 1% of the time, Pallas kernels for 0%

commit v1 on v0

v1 whole, which is shorter than its diff:
```python
import functools
import math

import jax
import jax.numpy as jnp
from jax import lax
from jax.experimental import pallas as pl
from jax.experimental.pallas import tpu as pltpu
from jax.sharding import PartitionSpec as P

HO = 8
HL = 10
ITERS = 3
STEP = 104
LANES = 128
courant = 2.0


def passed_along(value, axis, by):
    devices = lax.axis_size(axis)
    pairs = [(i, i + by) for i in range(devices) if 0 <= i + by < devices]
    return lax.ppermute(value, axis, pairs)


def from_behind(value, axis, steps):
    count = lax.axis_size(axis)
    pairs = [(source, (source + steps) % count) for source in range(count)]
    return lax.ppermute(value, axis, pairs)


def far(m):
    return ((-0.5 * m + 2.5) * m - 4.0) * m + 2.0


def near(m):
    return (1.5 * m - 2.5) * m * m + 1.0


def tap_weights(g):
    return [far(1.0 + g), near(g), near(1.0 - g), far(2.0 - g)]


def col_weights(h):
    w = [v.astype(jnp.bfloat16).astype(jnp.float32) for v in tap_weights(h)]
    tiny = 1.0 / 65536.0
    return [w[0], w[1] - w[0] * tiny, w[2], w[3] - w[2] * tiny]


def classes(start):
    groups = [(start + (3 - k)) >> 2 for k in range(4)]
    taps = [(groups[k] << 2) + k - start for k in range(4)]
    return groups, taps


def class_weights(taps, g):
    w = tap_weights(g)
    return [
        jnp.where(t == 0, w[0], jnp.where(t == 1, w[1], jnp.where(t == 2, w[2], w[3])))
        for t in taps
    ]


def window(parts, first, lane):
    block, off = divmod(first, LANES)
    if off == 0:
        return parts(block)
    a = pltpu.roll(parts(block), LANES - off, 1)
    b = pltpu.roll(parts(block + 1), LANES - off, 1)
    return jnp.where(lane < LANES - off, a, b)


def pick(table, idx):
    return jnp.take_along_axis(table, idx, axis=1, mode="promise_in_bounds")


def kernel(factor_ref, ext_ref, off_ref, out_ref, words, offs, inv, res):
    fields, rows_ext, levels, _ = ext_ref.shape
    _, rows, _, cols = out_ref.shape
    count = words.shape[2]
    lane = lax.broadcasted_iota(jnp.int32, (levels, LANES), 1)
    blocks = cols // LANES + 2

    def block_of(ref, *lead):
        return lambda i: ref[(*lead, slice(None), slice(i * LANES, (i + 1) * LANES))]

    for f in range(fields):
        def biggest(r, top):
            for i in range(blocks):
                top = jnp.maximum(top, jnp.abs(block_of(ext_ref, f, r)(i).astype(jnp.float32)))
            return top

        top = lax.fori_loop(0, rows_ext, biggest, jnp.zeros((levels, LANES), jnp.float32))
        top = jnp.maximum(jnp.max(top, axis=1, keepdims=True), 1e-30)
        power = jnp.floor(jnp.log(32000.0 / top) * (1.0 / math.log(2.0)))
        scale = jnp.broadcast_to(jnp.exp(power * math.log(2.0)), (levels, LANES))
        inv[f] = (1.0 / 65536.0) / scale

        def pack(r, _):
            def quantized(i):
                v = block_of(ext_ref, f, r)(i).astype(jnp.float32)
                return jnp.floor(v * scale + 0.5).astype(jnp.int32)

            memo = {}

            def part(i):
                if i not in memo:
                    memo[i] = quantized(i)
                return memo[i]

            for j in range(count):
                q = window(part, LANES - HO + STEP * j, lane)
                words[f, r, j] = (q << 16) + pltpu.roll(q, LANES - 1, 1)
            return 0

        lax.fori_loop(0, rows_ext, pack, 0)

    def windows_of(y, _):
        for c in range(2):
            for j in range(count):
                offs[c, y, j] = window(block_of(off_ref, c, y), LANES - HO + STEP * j, lane)
        return 0

    lax.fori_loop(0, rows, windows_of, 0)

    sy, dy, dx = factor_ref[rows], factor_ref[rows + 1], factor_ref[rows + 2]

    def stencil(f, row, j, idx, groups, masks, k, p):
        value = pick(words[f, row + k, j], idx[p])
        for g in range(1, groups):
            value = jnp.where(masks[k][g - 1], pick(words[f, row + 4 * g + k, j], idx[p]), value)
        return value.astype(jnp.float32), (value << 16).astype(jnp.float32)

    def point(i, _):
        y = i // count
        j = i - y * count
        oy = offs[0, y, j]
        ox = offs[1, y, j]
        oyf = oy.astype(jnp.float32)
        oxf = ox.astype(jnp.float32)
        my = oy >> 1
        mx = ox >> 1
        idx = [(lane + mx + (2 * p - 1)) & (LANES - 1) for p in range(2)]
        groups, taps = classes(my + 4)
        masks = [[groups[k] >= g for g in (1, 2)] for k in range(4)]
        wind = [
            [
                [v for p in range(2) for v in stencil(f, y + 5, j, idx, 3, masks, k, p)]
                for k in range(4)
            ]
            for f in range(2)
        ]
        sx = factor_ref[y]
        odd_y = (oy & 1).astype(jnp.float32)
        odd_x = (ox & 1).astype(jnp.float32)
        fy = jnp.full(oy.shape, 0.5, jnp.float32)
        fx = fy
        for _ in range(ITERS):
            cw = col_weights((odd_x + fx) * 0.5)
            rw = class_weights(taps, (odd_y + fy) * 0.5)
            mid = []
            for f in range(2):
                total = 0.0
                for k in range(4):
                    v = wind[f][k]
                    total += rw[k] * (cw[0] * v[0] + cw[1] * v[1] + cw[2] * v[2] + cw[3] * v[3])
                mid.append(total * inv[f])
            lx = dx * jnp.tanh(mid[0] * sx)
            ly = dy * jnp.tanh(mid[1] * sy)
            fy = 0.5 + 0.5 * jnp.tanh(0.5 * (ly - oyf - 0.5))
            fx = 0.5 + 0.5 * jnp.tanh(0.5 * (lx - oxf - 0.5))

        idx = [(lane + ox + (2 * p - 1)) & (LANES - 1) for p in range(2)]
        groups, taps = classes(oy + 8)
        masks = [[groups[k] >= g for g in (1, 2, 3, 4)] for k in range(4)]
        cw = col_weights(fx)
        rw = class_weights(taps, fy)
        for f in range(fields):
            total = 0.0
            for k in range(4):
                a = stencil(f, y + 1, j, idx, 5, masks, k, 0)
                b = stencil(f, y + 1, j, idx, 5, masks, k, 1)
                total += rw[k] * (cw[0] * a[0] + cw[1] * a[1] + cw[2] * b[0] + cw[3] * b[1])
            res[f, y, j] = total * inv[f]
        return 0

    lax.fori_loop(0, rows * count, point, 0)

    def merge(y, _):
        for f in range(fields):
            for m in range(cols // LANES):
                begin = m * LANES
                out = None
                for j in range(begin // STEP, (begin + LANES - 1) // STEP + 1):
                    moved = pltpu.roll(res[f, y, j], (STEP * j - HO - begin) % LANES, 1)
                    out = moved if out is None else jnp.where(lane >= STEP * j - begin, moved, out)
                out_ref[f, y, :, begin : begin + LANES] = out.astype(out_ref.dtype)
        return 0

    lax.fori_loop(0, rows, merge, 0)


def extend(fields):
    f, rows, levels, cols = fields.shape
    below = passed_along(fields[:, rows - HL :], "lat", 1)
    above = passed_along(fields[:, :HL], "lat", -1)
    tall = jnp.concatenate([below, fields, above], axis=1)
    count = rows + 2 * HL
    west_edge = jnp.moveaxis(tall[..., :HO], 3, 0).reshape(HO, f * count * levels)
    east_edge = jnp.moveaxis(tall[..., cols - HO :], 3, 0).reshape(HO, f * count * levels)
    west = from_behind(east_edge, "lon", 1).reshape(HO, f, count, levels)
    east = from_behind(west_edge, "lon", -1).reshape(HO, f, count, levels)
    blank = jnp.zeros((f, count, levels, LANES - HO), fields.dtype)
    return jnp.concatenate(
        [blank, jnp.moveaxis(west, 0, 3), tall, jnp.moveaxis(east, 0, 3), blank], axis=3
    )


def on_device(prognostic, halo_depth, cell_offsets):
    fields, levels, rows, cols = prognostic.shape
    ext = extend(jnp.transpose(prognostic, (0, 2, 1, 3)))
    off = jnp.pad(
        jnp.transpose(cell_offsets, (0, 2, 1, 3)), ((0, 0), (0, 0), (0, 0), (LANES, LANES))
    )
    lat_total = rows * lax.axis_size("lat")
    lat_index = (lax.axis_index("lat") * rows + jnp.arange(rows, dtype=jnp.int32)).astype(jnp.float32)
    coslat = jnp.cos((lat_index + 0.5) * (math.pi / lat_total) - 0.5 * math.pi)
    depth = halo_depth[:, 0, 0].astype(jnp.float32) - 1.0
    factor = jnp.concatenate(
        [-courant / (coslat * depth[1]), (-courant / depth[0])[None], depth]
    )
    count = -(-cols // STEP)
    moved = pl.pallas_call(
        kernel,
        out_shape=jax.ShapeDtypeStruct((fields, rows, levels, cols), jnp.bfloat16),
        in_specs=[
            pl.BlockSpec(memory_space=pltpu.SMEM),
            pl.BlockSpec(memory_space=pltpu.VMEM),
            pl.BlockSpec(memory_space=pltpu.VMEM),
        ],
        out_specs=pl.BlockSpec(memory_space=pltpu.VMEM),
        scratch_shapes=[
            pltpu.VMEM((fields, rows + 2 * HL, count, levels, LANES), jnp.int32),
            pltpu.VMEM((2, rows, count, levels, LANES), jnp.int32),
            pltpu.VMEM((fields, levels, LANES), jnp.float32),
            pltpu.VMEM((fields, rows, count, levels, LANES), jnp.float32),
        ],
        compiler_params=pltpu.CompilerParams(vmem_limit_bytes=40 * 2**20),
    )(factor, ext, off)
    return jnp.transpose(moved, (0, 2, 1, 3))


def solution(mesh):
    in_specs = (P(None, None, "lat", "lon"), P(None, "lat", "lon"), P(None, None, "lat", "lon"))
    out_specs = P(None, None, "lat", "lon")
    return jax.shard_map(
        on_device, mesh=mesh, in_specs=in_specs, out_specs=out_specs, check_vma=False
    )
```

time: 354 us -> 149 us (0.42); the launches traced: 350 us -> 149 us
  matrix products: 145 us -> 0 us
  local copies, waits for them, and re-layouts: 122 us -> 12.9 us
  Pallas kernels: 0 us -> 97.8 us
  loops' own time: 37.2 us -> 0 us
  other arithmetic: 27.8 us -> 1 us
  waiting for transfers between devices: 8.88 us -> 28.3 us
    dot_general x32 -> x0, matrix products: 145 us -> none  [band_sample(): jnp.einsum('ncrw,niw->ncri', windows, band_weight, preferred_element_type...]
    pallas_call x0 -> x1, Pallas kernels: none -> 97.8 us  [on_device(): pl.pallas_call(kernel, out_shape=jax.ShapeDtypeStruct((fields, rows, leve...]
    another operation x2 -> x0, loops' own time: 37.2 us -> none  [the longest x1 19.1 us: on_device(): lax.map(track_level, jnp.arange(levels, dtype=jnp.int32))]
    while x1040 -> x0, local copies, waits for them, and re-layouts: 36.1 us -> none
    dynamic_update_slice x24 -> x0, local copies, waits for them, and re-layouts: 33.6 us -> none  [the longest x16 28.3 us: on_device(): lax.map(track_level, jnp.arange(levels, dtype=jnp.int32))]
    ppermute x2, waiting for transfers between devices: 0.01 us -> 21.1 us  [from_behind(): return lax.ppermute(value, axis, pairs)]
    dynamic_slice x24 -> x0, local copies, waits for them, and re-layouts: 17.9 us -> none  [the longest x16 9.21 us: on_device(): lax.map(track_level, jnp.arange(levels, dtype=jnp.int32))]
    slice x19 -> x3, local copies, waits for them, and re-layouts: 16.4 us -> 0.94 us  [the longest x1 0.58 us: on_device(): depth[1]]
  transfers between devices with their start and end apart: 4 -> 4, of which waited for: 2 -> 4; matrix products, arithmetic and copies ran while one was open for 1% -> 2% of each run, Pallas kernels for 0% -> 0%
where the time goes in v1:
time: 149 us
  Pallas kernels  97.8 us (66%)
  waiting for transfers between devices  28.3 us (19%)
  local copies, waits for them, and re-layouts  12.9 us (9%)
  starting transfers between devices  7.91 us (5%)
    pallas_call x1, Pallas kernels, on_device(): pl.pallas_call(kernel, out_shape=jax.ShapeDtypeStruct((fields, rows, leve...  97.8 us
    ppermute x2, waiting for transfers between devices, from_behind(): return lax.ppermute(value, axis, pairs)  21.1 us
    ppermute x2, waiting for transfers between devices, passed_along(): return lax.ppermute(value, axis, pairs)  7.18 us
    ppermute x2, starting transfers between devices, passed_along(): return lax.ppermute(value, axis, pairs)  5.69 us
    concatenate x1, local copies, waits for them, and re-layouts, extend(): jnp.concatenate([blank, jnp.moveaxis(west, 0, 3), tall, jnp.moveaxis(east...  4.93 us
    unnamed x14, local copies, waits for them, and re-layouts  3.98 us
  transfers between devices with their start and end apart: 4, of which 4 were waited for; matrix products, arithmetic and copies ran while one was open for 2% of the time, Pallas kernels for 0%

profile of v1, /device:TPU:17, one launch (start us, length us, event | category | flops | bytes accessed | tf_op | source)
XLA Modules:
  0.0 148.6 jit_solution(4071565456624567049)
XLA Ops:
  0.0 0.0 copy-start.5
  0.0 1.7 %copy.9 = bf16[7,8,16,512]{3,1,2,0:T(8,128)(2,1)S(1)} copy(bf16[7,8,16,512]{3,2,1,0:T(8,128)(2,1)} %param.3) | data formatting | bytes 1835008 | tf_op args[0]
  1.7 0.1 fusion.2
  1.9 3.8 %collective-permute-start = (bf16[7,10,8,512]{3,2,1,0:T(8,128)(2,1)S(1)}, bf16[7,10,8,512]{3,2,1,0:T(8,128)(2,1)S(1)}, u32[]{:S(2)}, u32[]{:S(2)}) collective-permute-start(bf16[7,10,8,512]{3,2,1,0:T(8,128)(2,1)S(1)} %get-tuple-element.7), channel_id=1, source_target_pairs={{0,1},{1,2},{2,3},{3,4},{4,5},{5,6},{6,7},{8,9},{9,10},{10,11},{11... | collective-permute-start | bytes 1720328 | tf_op jit(solution)/shard_map/ppermute | solution.py:22
  5.6 1.9 %collective-permute-start.1 = (bf16[7,10,8,512]{3,2,1,0:T(8,128)(2,1)S(1)}, bf16[7,10,8,512]{3,2,1,0:T(8,128)(2,1)S(1)}, u32[]{:S(2)}, u32[]{:S(2)}) collective-permute-start(bf16[7,10,8,512]{3,2,1,0:T(8,128)(2,1)S(1)} %get-tuple-element.8), channel_id=1, source_target_pairs={{1,0},{2,1},{3,2},{4,3},{5,4},{6,5},{7,6},{9,8},{10,9},{11,10},{12... | collective-permute-start | bytes 1720328 | tf_op jit(solution)/shard_map/ppermute | solution.py:22
  7.6 0.0 copy-done.5
  7.6 0.6 fusion.3
  8.8 0.7 multiply_divide_fusion
  9.5 2.8 %collective-permute-done = bf16[7,10,8,512]{3,2,1,0:T(8,128)(2,1)S(1)} collective-permute-done((bf16[7,10,8,512]{3,2,1,0:T(8,128)(2,1)S(1)}, bf16[7,10,8,512]{3,2,1,0:T(8,128)(2,1)S(1)}, u32[]{:S(2)}, u32[]{:S(2)}) %collective-permute-start) | collective-permute-done | bytes 573472 | tf_op jit(solution)/shard_map/ppermute | solution.py:22
  12.3 4.4 %collective-permute-done.1 = bf16[7,10,8,512]{3,2,1,0:T(8,128)(2,1)S(1)} collective-permute-done((bf16[7,10,8,512]{3,2,1,0:T(8,128)(2,1)S(1)}, bf16[7,10,8,512]{3,2,1,0:T(8,128)(2,1)S(1)}, u32[]{:S(2)}, u32[]{:S(2)}) %collective-permute-start.1) | collective-permute-done | bytes 573472 | tf_op jit(solution)/shard_map/ppermute | solution.py:22
  16.7 0.2 pad_maximum_fusion
  16.9 0.0 copy-start.1
  16.9 0.0 copy-start.2
  16.9 0.2 fusion.1
  17.2 2.2 %collective-permute-start.3 = (bf16[8,2016]{0,1:T(8,128)(2,1)S(1)}, bf16[8,2016]{0,1:T(8,128)(2,1)S(1)}, u32[]{:S(2)}, u32[]{:S(2)}) collective-permute-start(bf16[8,2016]{0,1:T(8,128)(2,1)S(1)} %bitcast.30), channel_id=1, source_target_pairs={{0,24},{8,0},{16,8},{24,16},{1,25},{9,1},{17,9},{25,17},{2,26},{10... | collective-permute-start | bytes 96776 | tf_op jit(solution)/shard_map/ppermute | solution.py:28
  19.4 0.0 collective-permute-start.2
  19.4 0.1 pad_maximum_fusion.1.factor_ref
  19.5 0.0 copy-done.2
  19.5 0.3 copy.10
  19.8 0.9 pad.4.off_ref
  20.7 0.0 copy-done.1
  20.7 10.2 %collective-permute-done.3 = bf16[8,2016]{0,1:T(8,128)(2,1)S(1)} collective-permute-done((bf16[8,2016]{0,1:T(8,128)(2,1)S(1)}, bf16[8,2016]{0,1:T(8,128)(2,1)S(1)}, u32[]{:S(2)}, u32[]{:S(2)}) %collective-permute-start.3) | collective-permute-done | bytes 32288 | tf_op jit(solution)/shard_map/ppermute | solution.py:28
  31.0 0.0 copy-start.3
  31.0 10.9 %collective-permute-done.2 = bf16[8,2016]{0,1:T(8,128)(2,1)S(1)} collective-permute-done((bf16[8,2016]{0,1:T(8,128)(2,1)S(1)}, bf16[8,2016]{0,1:T(8,128)(2,1)S(1)}, u32[]{:S(2)}, u32[]{:S(2)}) %collective-permute-start.2) | collective-permute-done | bytes 32288 | tf_op jit(solution)/shard_map/ppermute | solution.py:28
  41.8 0.0 copy-start.4
  41.8 0.0 copy-done.3
  41.8 0.8 copy-done.4
  42.6 0.9 broadcast_in_dim.4
  43.5 4.9 %concatenate.11.ext_ref = bf16[7,36,8,768]{3,2,1,0:T(8,128)(2,1)S(1)} concatenate(bf16[7,36,8,120]{3,2,1,0:T(8,128)(2,1)} %broadcast_in_dim.4, bf16[7,36,8,8]{3,2,1,0:T(8,128)(2,1)} %bitcast.28, bf16[7,36,8,512]{3,2,1,0:T(8,128)(2,1)} %copy-done.1, bf16[7,36,8,8]{3,2,1,0:T(8,128)(2,1)} %bitcast.27, bf16[7,36,8,120]{3,2,1,0:T(8,128)(2,1)} %broadcast_in_dim.4), dimensions={3} | concatenate | bytes 6193152 | tf_op jit(solution)/shard_map/concatenate | solution.py:213
  48.4 0.0 copy-start
  48.4 1.1 copy-done
  49.6 97.8 %shard_map.37 = bf16[7,16,8,512]{3,2,1,0:T(8,128)(2,1)S(1)} custom-call(f32[19]{0:T(128)S(1)} %pad_maximum_fusion.1.factor_ref, bf16[7,36,8,768]{3,2,1,0:T(8,128)(2,1)S(1)} %concatenate.11.ext_ref, s32[2,16,8,768]{3,2,1,0:T(8,128)S(1)} %copy-done), custom_call_target="tpu_custom_call" | custom-call | tf_op jit(solution)/shard_map/pallas_call | solution.py:232
  147.4 1.2 copy.6
  (1 shorter events, 0.0 us)
Async XLA Ops:
  0.0 7.6 %copy-start.5 = (s32[2,1,1]{0,2,1:T(1,128)S(1)}, s32[2,1,1]{0,2,1:T(1,128)}, u32[]{:S(2)}) copy-start(s32[2,1,1]{0,2,1:T(1,128)} %param.4) | copy-start | bytes 28
  1.9 10.4 %collective-permute-start = (bf16[7,10,8,512]{3,2,1,0:T(8,128)(2,1)S(1)}, bf16[7,10,8,512]{3,2,1,0:T(8,128)(2,1)S(1)}, u32[]{:S(2)}, u32[]{:S(2)}) collective-permute-start(bf16[7,10,8,512]{3,2,1,0:T(8,128)(2,1)S(1)} %get-tuple-element.7), channel_id=1, source_target_pairs={{0,1},{1,2},{2,3},{3,4},{4,5},{5,6},{6,7},{8,9},{9,10},{10,11},{11... | collective-permute-start | bytes 1720328 | tf_op jit(solution)/shard_map/ppermute | solution.py:22
  5.6 11.0 %collective-permute-start.1 = (bf16[7,10,8,512]{3,2,1,0:T(8,128)(2,1)S(1)}, bf16[7,10,8,512]{3,2,1,0:T(8,128)(2,1)S(1)}, u32[]{:S(2)}, u32[]{:S(2)}) collective-permute-start(bf16[7,10,8,512]{3,2,1,0:T(8,128)(2,1)S(1)} %get-tuple-element.8), channel_id=1, source_target_pairs={{1,0},{2,1},{3,2},{4,3},{5,4},{6,5},{7,6},{9,8},{10,9},{11,10},{12... | collective-permute-start | bytes 1720328 | tf_op jit(solution)/shard_map/ppermute | solution.py:22
  16.9 3.8 %copy-start.1 = (bf16[7,36,8,512]{3,2,1,0:T(8,128)(2,1)}, bf16[7,36,8,512]{3,2,1,0:T(8,128)(2,1)S(1)}, u32[]{:S(2)}) copy-start(bf16[7,36,8,512]{3,2,1,0:T(8,128)(2,1)S(1)} %pad_maximum_fusion) | copy-start | bytes 6193156
  16.9 2.6 %copy-start.2 = (s32[2,8,16,512]{3,2,1,0:T(8,128)S(1)}, s32[2,8,16,512]{3,2,1,0:T(8,128)}, u32[]{:S(2)}) copy-start(s32[2,8,16,512]{3,2,1,0:T(8,128)} %param.5) | copy-start | bytes 1572868
  17.2 13.8 %collective-permute-start.3 = (bf16[8,2016]{0,1:T(8,128)(2,1)S(1)}, bf16[8,2016]{0,1:T(8,128)(2,1)S(1)}, u32[]{:S(2)}, u32[]{:S(2)}) collective-permute-start(bf16[8,2016]{0,1:T(8,128)(2,1)S(1)} %bitcast.30), channel_id=1, source_target_pairs={{0,24},{8,0},{16,8},{24,16},{1,25},{9,1},{17,9},{25,17},{2,26},{10... | collective-permute-start | bytes 96776 | tf_op jit(solution)/shard_map/ppermute | solution.py:28
  19.4 22.4 %collective-permute-start.2 = (bf16[8,2016]{0,1:T(8,128)(2,1)S(1)}, bf16[8,2016]{0,1:T(8,128)(2,1)S(1)}, u32[]{:S(2)}, u32[]{:S(2)}) collective-permute-start(bf16[8,2016]{0,1:T(8,128)(2,1)S(1)} %bitcast.29), channel_id=1, source_target_pairs={{0,8},{8,16},{16,24},{24,0},{1,9},{9,17},{17,25},{25,1},{2,10},{10... | collective-permute-start | bytes 96776 | tf_op jit(solution)/shard_map/ppermute | solution.py:28
  31.0 10.9 %copy-start.3 = (bf16[8,2016]{0,1:T(8,128)(2,1)}, bf16[8,2016]{0,1:T(8,128)(2,1)S(1)}, u32[]{:S(2)}) copy-start(bf16[8,2016]{0,1:T(8,128)(2,1)S(1)} %collective-permute-done.3) | copy-start | bytes 96772
  41.8 0.8 copy-start.4
  48.4 1.1 copy-start

commit v2 on v1

--- a/solution.py
+++ b/solution.py
@@ -73,7 +73,7 @@
     return jnp.take_along_axis(table, idx, axis=1, mode="promise_in_bounds")
 
 
-def kernel(factor_ref, ext_ref, off_ref, out_ref, words, offs, inv, res):
+def kernel(factor_ref, ext_ref, off_ref, out_ref, words, offs, inv, wind, frac, res):
     fields, rows_ext, levels, _ = ext_ref.shape
     _, rows, _, cols = out_ref.shape
     count = words.shape[2]
@@ -124,29 +124,41 @@
 
     sy, dy, dx = factor_ref[rows], factor_ref[rows + 1], factor_ref[rows + 2]
 
-    def stencil(f, row, j, idx, groups, masks, k, p):
-        value = pick(words[f, row + k, j], idx[p])
+    def gathered(f, row, j, idx, groups, masks, k):
+        value = pick(words[f, row + k, j], idx)
         for g in range(1, groups):
-            value = jnp.where(masks[k][g - 1], pick(words[f, row + 4 * g + k, j], idx[p]), value)
+            value = jnp.where(masks[k][g - 1], pick(words[f, row + 4 * g + k, j], idx), value)
+        return value
+
+    def split(value):
         return value.astype(jnp.float32), (value << 16).astype(jnp.float32)
 
-    def point(i, _):
+    def place(i):
         y = i // count
-        j = i - y * count
+        return y, i - y * count
+
+    def gather_wind(p):
+        def step(i, _):
+            y, j = place(i)
+            groups, _ = classes((offs[0, y, j] >> 1) + 4)
+            masks = [[groups[k] >= g for g in (1, 2)] for k in range(4)]
+            idx = (lane + (offs[1, y, j] >> 1) + (2 * p - 1)) & (LANES - 1)
+            for f in range(2):
+                for k in range(4):
+                    wind[i, f, k, p] = gathered(f, y + 5, j, idx, 3, masks, k)
+            return 0
+
+        lax.fori_loop(0, rows * count, step, 0)
+
+    def trajectory(i, _):
+        y, j = place(i)
         oy = offs[0, y, j]
         ox = offs[1, y, j]
         oyf = oy.astype(jnp.float32)
         oxf = ox.astype(jnp.float32)
-        my = oy >> 1
-        mx = ox >> 1
-        idx = [(lane + mx + (2 * p - 1)) & (LANES - 1) for p in range(2)]
-        groups, taps = classes(my + 4)
-        masks = [[groups[k] >= g for g in (1, 2)] for k in range(4)]
-        wind = [
-            [
-                [v for p in range(2) for v in stencil(f, y + 5, j, idx, 3, masks, k, p)]
-                for k in range(4)
-            ]
+        _, taps = classes((oy >> 1) + 4)
+        stencils = [
+            [[v for p in range(2) for v in split(wind[i, f, k, p])] for k in range(4)]
             for f in range(2)
         ]
         sx = factor_ref[y]
@@ -161,29 +173,42 @@
             for f in range(2):
                 total = 0.0
                 for k in range(4):
-                    v = wind[f][k]
+                    v = stencils[f][k]
                     total += rw[k] * (cw[0] * v[0] + cw[1] * v[1] + cw[2] * v[2] + cw[3] * v[3])
                 mid.append(total * inv[f])
             lx = dx * jnp.tanh(mid[0] * sx)
             ly = dy * jnp.tanh(mid[1] * sy)
             fy = 0.5 + 0.5 * jnp.tanh(0.5 * (ly - oyf - 0.5))
             fx = 0.5 + 0.5 * jnp.tanh(0.5 * (lx - oxf - 0.5))
-
-        idx = [(lane + ox + (2 * p - 1)) & (LANES - 1) for p in range(2)]
-        groups, taps = classes(oy + 8)
-        masks = [[groups[k] >= g for g in (1, 2, 3, 4)] for k in range(4)]
-        cw = col_weights(fx)
-        rw = class_weights(taps, fy)
-        for f in range(fields):
-            total = 0.0
-            for k in range(4):
-                a = stencil(f, y + 1, j, idx, 5, masks, k, 0)
-                b = stencil(f, y + 1, j, idx, 5, masks, k, 1)
-                total += rw[k] * (cw[0] * a[0] + cw[1] * a[1] + cw[2] * b[0] + cw[3] * b[1])
-            res[f, y, j] = total * inv[f]
+        frac[i, 0] = fy
+        frac[i, 1] = fx
         return 0
 
-    lax.fori_loop(0, rows * count, point, 0)
+    def advect(p):
+        def step(i, _):
+            y, j = place(i)
+            oy = offs[0, y, j]
+            idx = (lane + offs[1, y, j] + (2 * p - 1)) & (LANES - 1)
+            groups, taps = classes(oy + 8)
+            masks = [[groups[k] >= g for g in (1, 2, 3, 4)] for k in range(4)]
+            cw = col_weights(frac[i, 1])[2 * p : 2 * p + 2]
+            rw = class_weights(taps, frac[i, 0])
+            for f in range(fields):
+                total = 0.0
+                for k in range(4):
+                    a, b = split(gathered(f, y + 1, j, idx, 5, masks, k))
+                    total += rw[k] * (cw[0] * a + cw[1] * b)
+                total = total * inv[f]
+                res[f, y, j] = total if p == 0 else res[f, y, j] + total
+            return 0
+
+        lax.fori_loop(0, rows * count, step, 0)
+
+    gather_wind(0)
+    gather_wind(1)
+    lax.fori_loop(0, rows * count, trajectory, 0)
+    advect(0)
+    advect(1)
 
     def merge(y, _):
         for f in range(fields):
@@ -242,6 +267,8 @@
             pltpu.VMEM((fields, rows + 2 * HL, count, levels, LANES), jnp.int32),
             pltpu.VMEM((2, rows, count, levels, LANES), jnp.int32),
             pltpu.VMEM((fields, levels, LANES), jnp.float32),
+            pltpu.VMEM((rows * count, 2, 4, 2, levels, LANES), jnp.int32),
+            pltpu.VMEM((rows * count, 2, levels, LANES), jnp.float32),
             pltpu.VMEM((fields, rows, count, levels, LANES), jnp.float32),
         ],
         compiler_params=pltpu.CompilerParams(vmem_limit_bytes=40 * 2**20),

time: 149 us -> 162 us (1.087)
  Pallas kernels: 97.8 us -> 111 us
    pallas_call x1, Pallas kernels: 97.8 us -> 111 us  [on_device(): pl.pallas_call(kernel, out_shape=jax.ShapeDtypeStruct((fields, rows, leve...]
where the time goes in v2:
time: 162 us
  Pallas kernels  111 us (69%)
  waiting for transfers between devices  28.3 us (17%)
  local copies, waits for them, and re-layouts  12.9 us (8%)
  starting transfers between devices  7.91 us (5%)
    pallas_call x1, Pallas kernels, on_device(): pl.pallas_call(kernel, out_shape=jax.ShapeDtypeStruct((fields, rows, leve...  111 us
    ppermute x2, waiting for transfers between devices, from_behind(): return lax.ppermute(value, axis, pairs)  21.1 us
    ppermute x2, waiting for transfers between devices, passed_along(): return lax.ppermute(value, axis, pairs)  7.18 us
    ppermute x2, starting transfers between devices, passed_along(): return lax.ppermute(value, axis, pairs)  5.69 us
    concatenate x1, local copies, waits for them, and re-layouts, extend(): jnp.concatenate([blank, jnp.moveaxis(west, 0, 3), tall, jnp.moveaxis(east...  4.93 us
    unnamed x14, local copies, waits for them, and re-layouts  3.98 us
  transfers between devices with their start and end apart: 4, of which 4 were waited for; matrix products, arithmetic and copies ran while one was open for 2% of the time, Pallas kernels for 0%

profile of v2, /device:TPU:17, one launch (start us, length us, event | category | flops | bytes accessed | tf_op | source)
XLA Modules:
  0.0 162.0 jit_solution(11235523856683482979)
XLA Ops:
  0.0 0.0 copy-start.5
  0.0 1.7 %copy.9 = bf16[7,8,16,512]{3,1,2,0:T(8,128)(2,1)S(1)} copy(bf16[7,8,16,512]{3,2,1,0:T(8,128)(2,1)} %param.3) | data formatting | bytes 1835008 | tf_op args[0]
  1.7 0.1 fusion.2
  1.9 3.8 %collective-permute-start = (bf16[7,10,8,512]{3,2,1,0:T(8,128)(2,1)S(1)}, bf16[7,10,8,512]{3,2,1,0:T(8,128)(2,1)S(1)}, u32[]{:S(2)}, u32[]{:S(2)}) collective-permute-start(bf16[7,10,8,512]{3,2,1,0:T(8,128)(2,1)S(1)} %get-tuple-element.7), channel_id=1, source_target_pairs={{0,1},{1,2},{2,3},{3,4},{4,5},{5,6},{6,7},{8,9},{9,10},{10,11},{11... | collective-permute-start | bytes 1720328 | tf_op jit(solution)/shard_map/ppermute | solution.py:22
  5.6 1.9 %collective-permute-start.1 = (bf16[7,10,8,512]{3,2,1,0:T(8,128)(2,1)S(1)}, bf16[7,10,8,512]{3,2,1,0:T(8,128)(2,1)S(1)}, u32[]{:S(2)}, u32[]{:S(2)}) collective-permute-start(bf16[7,10,8,512]{3,2,1,0:T(8,128)(2,1)S(1)} %get-tuple-element.8), channel_id=1, source_target_pairs={{1,0},{2,1},{3,2},{4,3},{5,4},{6,5},{7,6},{9,8},{10,9},{11,10},{12... | collective-permute-start | bytes 1720328 | tf_op jit(solution)/shard_map/ppermute | solution.py:22
  7.6 0.0 copy-done.5
  7.6 0.6 fusion.3
  8.8 0.7 multiply_divide_fusion
  9.5 2.8 %collective-permute-done = bf16[7,10,8,512]{3,2,1,0:T(8,128)(2,1)S(1)} collective-permute-done((bf16[7,10,8,512]{3,2,1,0:T(8,128)(2,1)S(1)}, bf16[7,10,8,512]{3,2,1,0:T(8,128)(2,1)S(1)}, u32[]{:S(2)}, u32[]{:S(2)}) %collective-permute-start) | collective-permute-done | bytes 573472 | tf_op jit(solution)/shard_map/ppermute | solution.py:22
  12.3 4.4 %collective-permute-done.1 = bf16[7,10,8,512]{3,2,1,0:T(8,128)(2,1)S(1)} collective-permute-done((bf16[7,10,8,512]{3,2,1,0:T(8,128)(2,1)S(1)}, bf16[7,10,8,512]{3,2,1,0:T(8,128)(2,1)S(1)}, u32[]{:S(2)}, u32[]{:S(2)}) %collective-permute-start.1) | collective-permute-done | bytes 573472 | tf_op jit(solution)/shard_map/ppermute | solution.py:22
  16.7 0.2 pad_maximum_fusion
  16.9 0.0 copy-start.1
  16.9 0.0 copy-start.2
  16.9 0.2 fusion.1
  17.2 2.2 %collective-permute-start.3 = (bf16[8,2016]{0,1:T(8,128)(2,1)S(1)}, bf16[8,2016]{0,1:T(8,128)(2,1)S(1)}, u32[]{:S(2)}, u32[]{:S(2)}) collective-permute-start(bf16[8,2016]{0,1:T(8,128)(2,1)S(1)} %bitcast.30), channel_id=1, source_target_pairs={{0,24},{8,0},{16,8},{24,16},{1,25},{9,1},{17,9},{25,17},{2,26},{10... | collective-permute-start | bytes 96776 | tf_op jit(solution)/shard_map/ppermute | solution.py:28
  19.4 0.0 collective-permute-start.2
  19.4 0.1 pad_maximum_fusion.1.factor_ref
  19.5 0.0 copy-done.2
  19.5 0.3 copy.10
  19.8 0.9 pad.4.off_ref
  20.7 0.0 copy-done.1
  20.7 10.2 %collective-permute-done.3 = bf16[8,2016]{0,1:T(8,128)(2,1)S(1)} collective-permute-done((bf16[8,2016]{0,1:T(8,128)(2,1)S(1)}, bf16[8,2016]{0,1:T(8,128)(2,1)S(1)}, u32[]{:S(2)}, u32[]{:S(2)}) %collective-permute-start.3) | collective-permute-done | bytes 32288 | tf_op jit(solution)/shard_map/ppermute | solution.py:28
  31.0 0.0 copy-start.3
  31.0 10.9 %collective-permute-done.2 = bf16[8,2016]{0,1:T(8,128)(2,1)S(1)} collective-permute-done((bf16[8,2016]{0,1:T(8,128)(2,1)S(1)}, bf16[8,2016]{0,1:T(8,128)(2,1)S(1)}, u32[]{:S(2)}, u32[]{:S(2)}) %collective-permute-start.2) | collective-permute-done | bytes 32288 | tf_op jit(solution)/shard_map/ppermute | solution.py:28
  41.8 0.0 copy-start.4
  41.8 0.0 copy-done.3
  41.8 0.8 copy-done.4
  42.6 0.9 broadcast_in_dim.4
  43.5 4.9 %concatenate.11.ext_ref = bf16[7,36,8,768]{3,2,1,0:T(8,128)(2,1)S(1)} concatenate(bf16[7,36,8,120]{3,2,1,0:T(8,128)(2,1)} %broadcast_in_dim.4, bf16[7,36,8,8]{3,2,1,0:T(8,128)(2,1)} %bitcast.28, bf16[7,36,8,512]{3,2,1,0:T(8,128)(2,1)} %copy-done.1, bf16[7,36,8,8]{3,2,1,0:T(8,128)(2,1)} %bitcast.27, bf16[7,36,8,120]{3,2,1,0:T(8,128)(2,1)} %broadcast_in_dim.4), dimensions={3} | concatenate | bytes 6193152 | tf_op jit(solution)/shard_map/concatenate | solution.py:238
  48.4 0.0 copy-start
  48.4 1.1 copy-done
  49.6 111.2 %shard_map.37 = bf16[7,16,8,512]{3,2,1,0:T(8,128)(2,1)S(1)} custom-call(f32[19]{0:T(128)S(1)} %pad_maximum_fusion.1.factor_ref, bf16[7,36,8,768]{3,2,1,0:T(8,128)(2,1)S(1)} %concatenate.11.ext_ref, s32[2,16,8,768]{3,2,1,0:T(8,128)S(1)} %copy-done), custom_call_target="tpu_custom_call" | custom-call | tf_op jit(solution)/shard_map/pallas_call | solution.py:257
  160.8 1.2 copy.6
  (1 shorter events, 0.0 us)
Async XLA Ops:
  0.0 7.6 %copy-start.5 = (s32[2,1,1]{0,2,1:T(1,128)S(1)}, s32[2,1,1]{0,2,1:T(1,128)}, u32[]{:S(2)}) copy-start(s32[2,1,1]{0,2,1:T(1,128)} %param.4) | copy-start | bytes 28
  1.9 10.4 %collective-permute-start = (bf16[7,10,8,512]{3,2,1,0:T(8,128)(2,1)S(1)}, bf16[7,10,8,512]{3,2,1,0:T(8,128)(2,1)S(1)}, u32[]{:S(2)}, u32[]{:S(2)}) collective-permute-start(bf16[7,10,8,512]{3,2,1,0:T(8,128)(2,1)S(1)} %get-tuple-element.7), channel_id=1, source_target_pairs={{0,1},{1,2},{2,3},{3,4},{4,5},{5,6},{6,7},{8,9},{9,10},{10,11},{11... | collective-permute-start | bytes 1720328 | tf_op jit(solution)/shard_map/ppermute | solution.py:22
  5.6 11.0 %collective-permute-start.1 = (bf16[7,10,8,512]{3,2,1,0:T(8,128)(2,1)S(1)}, bf16[7,10,8,512]{3,2,1,0:T(8,128)(2,1)S(1)}, u32[]{:S(2)}, u32[]{:S(2)}) collective-permute-start(bf16[7,10,8,512]{3,2,1,0:T(8,128)(2,1)S(1)} %get-tuple-element.8), channel_id=1, source_target_pairs={{1,0},{2,1},{3,2},{4,3},{5,4},{6,5},{7,6},{9,8},{10,9},{11,10},{12... | collective-permute-start | bytes 1720328 | tf_op jit(solution)/shard_map/ppermute | solution.py:22
  16.9 3.8 %copy-start.1 = (bf16[7,36,8,512]{3,2,1,0:T(8,128)(2,1)}, bf16[7,36,8,512]{3,2,1,0:T(8,128)(2,1)S(1)}, u32[]{:S(2)}) copy-start(bf16[7,36,8,512]{3,2,1,0:T(8,128)(2,1)S(1)} %pad_maximum_fusion) | copy-start | bytes 6193156
  16.9 2.6 %copy-start.2 = (s32[2,8,16,512]{3,2,1,0:T(8,128)S(1)}, s32[2,8,16,512]{3,2,1,0:T(8,128)}, u32[]{:S(2)}) copy-start(s32[2,8,16,512]{3,2,1,0:T(8,128)} %param.5) | copy-start | bytes 1572868
  17.2 13.8 %collective-permute-start.3 = (bf16[8,2016]{0,1:T(8,128)(2,1)S(1)}, bf16[8,2016]{0,1:T(8,128)(2,1)S(1)}, u32[]{:S(2)}, u32[]{:S(2)}) collective-permute-start(bf16[8,2016]{0,1:T(8,128)(2,1)S(1)} %bitcast.30), channel_id=1, source_target_pairs={{0,24},{8,0},{16,8},{24,16},{1,25},{9,1},{17,9},{25,17},{2,26},{10... | collective-permute-start | bytes 96776 | tf_op jit(solution)/shard_map/ppermute | solution.py:28
  19.4 22.4 %collective-permute-start.2 = (bf16[8,2016]{0,1:T(8,128)(2,1)S(1)}, bf16[8,2016]{0,1:T(8,128)(2,1)S(1)}, u32[]{:S(2)}, u32[]{:S(2)}) collective-permute-start(bf16[8,2016]{0,1:T(8,128)(2,1)S(1)} %bitcast.29), channel_id=1, source_target_pairs={{0,8},{8,16},{16,24},{24,0},{1,9},{9,17},{17,25},{25,1},{2,10},{10... | collective-permute-start | bytes 96776 | tf_op jit(solution)/shard_map/ppermute | solution.py:28
  31.0 10.9 %copy-start.3 = (bf16[8,2016]{0,1:T(8,128)(2,1)}, bf16[8,2016]{0,1:T(8,128)(2,1)S(1)}, u32[]{:S(2)}) copy-start(bf16[8,2016]{0,1:T(8,128)(2,1)S(1)} %collective-permute-done.3) | copy-start | bytes 96772
  41.8 0.8 copy-start.4
  48.4 1.1 copy-start

commit v3 on v1

--- a/solution.py
+++ b/solution.py
@@ -73,20 +73,34 @@
     return jnp.take_along_axis(table, idx, axis=1, mode="promise_in_bounds")
 
 
-def kernel(factor_ref, ext_ref, off_ref, out_ref, words, offs, inv, res):
+def kernel(factor_ref, west_ref, ext_ref, east_ref, off_ref, out_ref, words, offs, inv, res):
     fields, rows_ext, levels, _ = ext_ref.shape
     _, rows, _, cols = out_ref.shape
     count = words.shape[2]
     lane = lax.broadcasted_iota(jnp.int32, (levels, LANES), 1)
     blocks = cols // LANES + 2
 
-    def block_of(ref, *lead):
-        return lambda i: ref[(*lead, slice(None), slice(i * LANES, (i + 1) * LANES))]
+    def block_of(f, r):
+        def block(i):
+            if i == 0:
+                return west_ref[f, r]
+            if i == blocks - 1:
+                return east_ref[f, r]
+            return ext_ref[f, r, :, (i - 1) * LANES : i * LANES]
+
+        return block
+
+    def offsets_of(c, y):
+        def block(i):
+            i = min(max(i, 1), blocks - 2)
+            return off_ref[c, y, :, (i - 1) * LANES : i * LANES]
+
+        return block
 
     for f in range(fields):
         def biggest(r, top):
             for i in range(blocks):
-                top = jnp.maximum(top, jnp.abs(block_of(ext_ref, f, r)(i).astype(jnp.float32)))
+                top = jnp.maximum(top, jnp.abs(block_of(f, r)(i).astype(jnp.float32)))
             return top
 
         top = lax.fori_loop(0, rows_ext, biggest, jnp.zeros((levels, LANES), jnp.float32))
@@ -97,7 +111,7 @@
 
         def pack(r, _):
             def quantized(i):
-                v = block_of(ext_ref, f, r)(i).astype(jnp.float32)
+                v = block_of(f, r)(i).astype(jnp.float32)
                 return jnp.floor(v * scale + 0.5).astype(jnp.int32)
 
             memo = {}
@@ -117,7 +131,7 @@
     def windows_of(y, _):
         for c in range(2):
             for j in range(count):
-                offs[c, y, j] = window(block_of(off_ref, c, y), LANES - HO + STEP * j, lane)
+                offs[c, y, j] = window(offsets_of(c, y), LANES - HO + STEP * j, lane)
         return 0
 
     lax.fori_loop(0, rows, windows_of, 0)
@@ -204,23 +218,15 @@
     below = passed_along(fields[:, rows - HL :], "lat", 1)
     above = passed_along(fields[:, :HL], "lat", -1)
     tall = jnp.concatenate([below, fields, above], axis=1)
-    count = rows + 2 * HL
-    west_edge = jnp.moveaxis(tall[..., :HO], 3, 0).reshape(HO, f * count * levels)
-    east_edge = jnp.moveaxis(tall[..., cols - HO :], 3, 0).reshape(HO, f * count * levels)
-    west = from_behind(east_edge, "lon", 1).reshape(HO, f, count, levels)
-    east = from_behind(west_edge, "lon", -1).reshape(HO, f, count, levels)
-    blank = jnp.zeros((f, count, levels, LANES - HO), fields.dtype)
-    return jnp.concatenate(
-        [blank, jnp.moveaxis(west, 0, 3), tall, jnp.moveaxis(east, 0, 3), blank], axis=3
-    )
+    west = from_behind(tall[..., cols - LANES :], "lon", 1)
+    east = from_behind(tall[..., :LANES], "lon", -1)
+    return west, tall, east
 
 
 def on_device(prognostic, halo_depth, cell_offsets):
     fields, levels, rows, cols = prognostic.shape
-    ext = extend(jnp.transpose(prognostic, (0, 2, 1, 3)))
-    off = jnp.pad(
-        jnp.transpose(cell_offsets, (0, 2, 1, 3)), ((0, 0), (0, 0), (0, 0), (LANES, LANES))
-    )
+    west, tall, east = extend(jnp.transpose(prognostic, (0, 2, 1, 3)))
+    off = jnp.transpose(cell_offsets, (0, 2, 1, 3))
     lat_total = rows * lax.axis_size("lat")
     lat_index = (lax.axis_index("lat") * rows + jnp.arange(rows, dtype=jnp.int32)).astype(jnp.float32)
     coslat = jnp.cos((lat_index + 0.5) * (math.pi / lat_total) - 0.5 * math.pi)
@@ -236,6 +242,8 @@
             pl.BlockSpec(memory_space=pltpu.SMEM),
             pl.BlockSpec(memory_space=pltpu.VMEM),
             pl.BlockSpec(memory_space=pltpu.VMEM),
+            pl.BlockSpec(memory_space=pltpu.VMEM),
+            pl.BlockSpec(memory_space=pltpu.VMEM),
         ],
         out_specs=pl.BlockSpec(memory_space=pltpu.VMEM),
         scratch_shapes=[
@@ -245,7 +253,7 @@
             pltpu.VMEM((fields, rows, count, levels, LANES), jnp.float32),
         ],
         compiler_params=pltpu.CompilerParams(vmem_limit_bytes=40 * 2**20),
-    )(factor, ext, off)
+    )(factor, west, tall, east, off)
     return jnp.transpose(moved, (0, 2, 1, 3))
 
 

time: 149 us -> 142 us (0.953)
  local copies, waits for them, and re-layouts: 12.9 us -> 5.17 us
    concatenate x1 -> x0, local copies, waits for them, and re-layouts: 4.93 us -> none  [extend(): jnp.concatenate([blank, jnp.moveaxis(west, 0, 3), tall, jnp.moveaxis(east...]
    unnamed x14 -> x4, local copies, waits for them, and re-layouts: 3.98 us -> 3.07 us
where the time goes in v3:
time: 142 us
  Pallas kernels  97.8 us (69%)
  waiting for transfers between devices  27.9 us (20%)
  starting transfers between devices  8.1 us (6%)
  local copies, waits for them, and re-layouts  5.17 us (4%)
  other arithmetic  2.07 us (1%)
    pallas_call x1, Pallas kernels, on_device(): pl.pallas_call(kernel, out_shape=jax.ShapeDtypeStruct((fields, rows, leve...  97.8 us
    ppermute x2, waiting for transfers between devices, from_behind(): return lax.ppermute(value, axis, pairs)  20 us
    ppermute x2, waiting for transfers between devices, passed_along(): return lax.ppermute(value, axis, pairs)  7.85 us
    ppermute x2, starting transfers between devices, passed_along(): return lax.ppermute(value, axis, pairs)  5.69 us
    unnamed x4, local copies, waits for them, and re-layouts  3.07 us
  transfers between devices with their start and end apart: 4, of which 4 were waited for; matrix products, arithmetic and copies ran while one was open for 2% of the time, Pallas kernels for 0%

profile of v3, /device:TPU:17, one launch (start us, length us, event | category | flops | bytes accessed | tf_op | source)
XLA Modules:
  0.0 141.8 jit_solution(2637060254954417510)
XLA Ops:
  0.0 1.7 %copy.9 = bf16[7,8,16,512]{3,1,2,0:T(8,128)(2,1)S(1)} copy(bf16[7,8,16,512]{3,2,1,0:T(8,128)(2,1)} %param.3) | data formatting | bytes 1835008 | tf_op args[0]
  1.7 0.1 fusion.2
  1.8 3.8 %collective-permute-start = (bf16[7,10,8,512]{3,2,1,0:T(8,128)(2,1)S(1)}, bf16[7,10,8,512]{3,2,1,0:T(8,128)(2,1)S(1)}, u32[]{:S(2)}, u32[]{:S(2)}) collective-permute-start(bf16[7,10,8,512]{3,2,1,0:T(8,128)(2,1)S(1)} %get-tuple-element.7), channel_id=1, source_target_pairs={{0,1},{1,2},{2,3},{3,4},{4,5},{5,6},{6,7},{8,9},{9,10},{10,11},{11... | collective-permute-start | bytes 1720328 | tf_op jit(solution)/shard_map/ppermute | solution.py:22
  5.6 1.9 %collective-permute-start.1 = (bf16[7,10,8,512]{3,2,1,0:T(8,128)(2,1)S(1)}, bf16[7,10,8,512]{3,2,1,0:T(8,128)(2,1)}, u32[]{:S(2)}, u32[]{:S(2)}) collective-permute-start(bf16[7,10,8,512]{3,2,1,0:T(8,128)(2,1)S(1)} %get-tuple-element.8), channel_id=1, source_target_pairs={{1,0},{2,1},{3,2},{4,3},{5,4},{6,5},{7,6},{9,8},{10,9},{11,10},{12... | collective-permute-start | bytes 1720328 | tf_op jit(solution)/shard_map/ppermute | solution.py:22
  7.5 1.4 copy.10
  8.9 3.3 %collective-permute-done = bf16[7,10,8,512]{3,2,1,0:T(8,128)(2,1)S(1)} collective-permute-done((bf16[7,10,8,512]{3,2,1,0:T(8,128)(2,1)S(1)}, bf16[7,10,8,512]{3,2,1,0:T(8,128)(2,1)S(1)}, u32[]{:S(2)}, u32[]{:S(2)}) %collective-permute-start) | collective-permute-done | bytes 573472 | tf_op jit(solution)/shard_map/ppermute | solution.py:22
  12.2 4.5 %collective-permute-done.1 = bf16[7,10,8,512]{3,2,1,0:T(8,128)(2,1)} collective-permute-done((bf16[7,10,8,512]{3,2,1,0:T(8,128)(2,1)S(1)}, bf16[7,10,8,512]{3,2,1,0:T(8,128)(2,1)}, u32[]{:S(2)}, u32[]{:S(2)}) %collective-permute-start.1) | collective-permute-done | bytes 573472 | tf_op jit(solution)/shard_map/ppermute | solution.py:22
  16.7 1.3 pad_maximum_fusion.ext_ref
  18.0 0.0 copy-start
  18.0 0.2 fusion.1
  18.2 1.3 collective-permute-start.2
  19.5 1.2 collective-permute-start.3
  20.7 0.0 copy-done
  20.7 0.6 fusion.3
  22.0 0.7 multiply_divide_fusion
  22.7 0.1 pad_maximum_fusion.1.factor_ref
  22.7 9.9 %collective-permute-done.2.west_ref = bf16[7,36,8,128]{3,2,1,0:T(8,128)(2,1)S(1)} collective-permute-done((bf16[7,36,8,128]{3,2,1,0:T(8,128)(2,1)S(1)}, bf16[7,36,8,128]{3,2,1,0:T(8,128)(2,1)S(1)}, u32[]{:S(2)}, u32[]{:S(2)}) %collective-permute-start.2) | collective-permute-done | bytes 516128 | tf_op jit(solution)/shard_map/ppermute | solution.py:28
  32.7 10.1 %collective-permute-done.3.east_ref = bf16[7,36,8,128]{3,2,1,0:T(8,128)(2,1)S(1)} collective-permute-done((bf16[7,36,8,128]{3,2,1,0:T(8,128)(2,1)S(1)}, bf16[7,36,8,128]{3,2,1,0:T(8,128)(2,1)S(1)}, u32[]{:S(2)}, u32[]{:S(2)}) %collective-permute-start.3) | collective-permute-done | bytes 516128 | tf_op jit(solution)/shard_map/ppermute | solution.py:28
  42.8 97.8 %shard_map.37 = bf16[7,16,8,512]{3,2,1,0:T(8,128)(2,1)S(1)} custom-call(f32[19]{0:T(128)S(1)} %pad_maximum_fusion.1.factor_ref, bf16[7,36,8,128]{3,2,1,0:T(8,128)(2,1)S(1)} %collective-permute-done.2.west_ref, bf16[7,36,8,512]{3,2,1,0:T(8,128)(2,1)S(1)} %pad_maximum_fusion.ext_ref, bf16[7,36,8,128]{3,2,1,0:T(8,128)(2,1)S(1)} %collective-permute-done.3.east_ref, ...), custom_call_target="tpu_custom_call" | custom-call | tf_op jit(solution)/shard_map/pallas_call | solution.py:238
  140.6 1.2 copy.6
  (1 shorter events, 0.0 us)
Async XLA Ops:
  1.8 10.4 %collective-permute-start = (bf16[7,10,8,512]{3,2,1,0:T(8,128)(2,1)S(1)}, bf16[7,10,8,512]{3,2,1,0:T(8,128)(2,1)S(1)}, u32[]{:S(2)}, u32[]{:S(2)}) collective-permute-start(bf16[7,10,8,512]{3,2,1,0:T(8,128)(2,1)S(1)} %get-tuple-element.7), channel_id=1, source_target_pairs={{0,1},{1,2},{2,3},{3,4},{4,5},{5,6},{6,7},{8,9},{9,10},{10,11},{11... | collective-permute-start | bytes 1720328 | tf_op jit(solution)/shard_map/ppermute | solution.py:22
  5.6 11.1 %collective-permute-start.1 = (bf16[7,10,8,512]{3,2,1,0:T(8,128)(2,1)S(1)}, bf16[7,10,8,512]{3,2,1,0:T(8,128)(2,1)}, u32[]{:S(2)}, u32[]{:S(2)}) collective-permute-start(bf16[7,10,8,512]{3,2,1,0:T(8,128)(2,1)S(1)} %get-tuple-element.8), channel_id=1, source_target_pairs={{1,0},{2,1},{3,2},{4,3},{5,4},{6,5},{7,6},{9,8},{10,9},{11,10},{12... | collective-permute-start | bytes 1720328 | tf_op jit(solution)/shard_map/ppermute | solution.py:22
  18.0 2.6 %copy-start = (s32[2,1,1]{0,2,1:T(1,128)S(1)}, s32[2,1,1]{0,2,1:T(1,128)}, u32[]{:S(2)}) copy-start(s32[2,1,1]{0,2,1:T(1,128)} %param.4) | copy-start | bytes 28
  18.2 14.4 %collective-permute-start.2 = (bf16[7,36,8,128]{3,2,1,0:T(8,128)(2,1)S(1)}, bf16[7,36,8,128]{3,2,1,0:T(8,128)(2,1)S(1)}, u32[]{:S(2)}, u32[]{:S(2)}) collective-permute-start(bf16[7,36,8,128]{3,2,1,0:T(8,128)(2,1)S(1)} %get-tuple-element.6), channel_id=1, source_target_pairs={{0,8},{8,16},{16,24},{24,0},{1,9},{9,17},{17,25},{25,1},{2,10},{10... | collective-permute-start | bytes 1548296 | tf_op jit(solution)/shard_map/ppermute | solution.py:28
  19.5 23.3 %collective-permute-start.3 = (bf16[7,36,8,128]{3,2,1,0:T(8,128)(2,1)S(1)}, bf16[7,36,8,128]{3,2,1,0:T(8,128)(2,1)S(1)}, u32[]{:S(2)}, u32[]{:S(2)}) collective-permute-start(bf16[7,36,8,128]{3,2,1,0:T(8,128)(2,1)S(1)} %get-tuple-element.5), channel_id=1, source_target_pairs={{0,24},{8,0},{16,8},{24,16},{1,25},{9,1},{17,9},{25,17},{2,26},{10... | collective-permute-start | bytes 1548296 | tf_op jit(solution)/shard_map/ppermute | solution.py:28

commit v4 on v3

--- a/solution.py
+++ b/solution.py
@@ -218,8 +218,15 @@
     below = passed_along(fields[:, rows - HL :], "lat", 1)
     above = passed_along(fields[:, :HL], "lat", -1)
     tall = jnp.concatenate([below, fields, above], axis=1)
-    west = from_behind(tall[..., cols - LANES :], "lon", 1)
-    east = from_behind(tall[..., :LANES], "lon", -1)
+    outer = jnp.concatenate([below, above], axis=1)
+
+    def beside(lanes, steps):
+        own = from_behind(fields[..., lanes], "lon", steps)
+        halo = from_behind(outer[..., lanes], "lon", steps)
+        return jnp.concatenate([halo[:, :HL], own, halo[:, HL:]], axis=1)
+
+    west = beside(slice(cols - LANES, cols), 1)
+    east = beside(slice(0, LANES), -1)
     return west, tall, east
 
 

time: 142 us -> 134 us (0.944)
  waiting for transfers between devices: 27.9 us -> 16.8 us
  starting transfers between devices: 8.1 us -> 10.1 us
    ppermute x2 -> x4, waiting for transfers between devices: 20 us -> 10.9 us  [from_behind(): return lax.ppermute(value, axis, pairs)]
    ppermute x2, waiting for transfers between devices: 7.85 us -> 5.84 us  [passed_along(): return lax.ppermute(value, axis, pairs)]
    concatenate x0 -> x2, other arithmetic: none -> 2 us  [beside(): return jnp.concatenate([halo[:, :HL], own, halo[:, HL:]], axis=1)]
    ppermute x2 -> x4, starting transfers between devices: 2.42 us -> 4.39 us  [from_behind(): return lax.ppermute(value, axis, pairs)]
    unnamed x4 -> x7, local copies, waits for them, and re-layouts: 3.07 us -> 2.07 us
  transfers between devices with their start and end apart: 4 -> 6, of which waited for: 4 -> 4; matrix products, arithmetic and copies ran while one was open for 2% -> 3% of each run, Pallas kernels for 0% -> 0%
where the time goes in v4:
time: 134 us; the launch traced here: 133 us
  Pallas kernels  97.8 us (73%)
  waiting for transfers between devices  16.8 us (13%)
  starting transfers between devices  10.1 us (8%)
  local copies, waits for them, and re-layouts  5.01 us (4%)
  other arithmetic  2.99 us (2%)
    pallas_call x1, Pallas kernels, on_device(): pl.pallas_call(kernel, out_shape=jax.ShapeDtypeStruct((fields, rows, leve...  97.8 us
    ppermute x4, waiting for transfers between devices, from_behind(): return lax.ppermute(value, axis, pairs)  10.9 us
    ppermute x2, waiting for transfers between devices, passed_along(): return lax.ppermute(value, axis, pairs)  5.84 us
    ppermute x2, starting transfers between devices, passed_along(): return lax.ppermute(value, axis, pairs)  5.69 us
    ppermute x4, starting transfers between devices, from_behind(): return lax.ppermute(value, axis, pairs)  4.39 us
  transfers between devices with their start and end apart: 6, of which 4 were waited for; matrix products, arithmetic and copies ran while one was open for 3% of the time, Pallas kernels for 0%

profile of v4, /device:TPU:17, one launch (start us, length us, event | category | flops | bytes accessed | tf_op | source)
XLA Modules:
  0.0 133.4 jit_solution(10524535440746687500)
XLA Ops:
  0.0 1.7 %copy.9 = bf16[7,8,16,512]{3,1,2,0:T(8,128)(2,1)S(1)} copy(bf16[7,8,16,512]{3,2,1,0:T(8,128)(2,1)} %param.3) | data formatting | bytes 1835008 | tf_op args[0]
  1.7 0.0 copy-start.1
  1.7 0.1 fusion.3
  1.8 3.8 %collective-permute-start = (bf16[7,10,8,512]{3,2,1,0:T(8,128)(2,1)S(1)}, bf16[7,10,8,512]{3,2,1,0:T(8,128)(2,1)S(1)}, u32[]{:S(2)}, u32[]{:S(2)}) collective-permute-start(bf16[7,10,8,512]{3,2,1,0:T(8,128)(2,1)S(1)} %get-tuple-element.10), channel_id=1, source_target_pairs={{0,1},{1,2},{2,3},{3,4},{4,5},{5,6},{6,7},{8,9},{9,10},{10,11},{11... | collective-permute-start | bytes 1720328 | tf_op jit(solution)/shard_map/ppermute | solution.py:22
  5.6 1.9 %collective-permute-start.1 = (bf16[7,10,8,512]{3,2,1,0:T(8,128)(2,1)S(1)}, bf16[7,10,8,512]{3,2,1,0:T(8,128)(2,1)S(1)}, u32[]{:S(2)}, u32[]{:S(2)}) collective-permute-start(bf16[7,10,8,512]{3,2,1,0:T(8,128)(2,1)S(1)} %get-tuple-element.9), channel_id=1, source_target_pairs={{1,0},{2,1},{3,2},{4,3},{5,4},{6,5},{7,6},{9,8},{10,9},{11,10},{12... | collective-permute-start | bytes 1720328 | tf_op jit(solution)/shard_map/ppermute | solution.py:22
  7.5 0.8 fusion.2
  8.4 2.2 %collective-permute-start.5 = (bf16[7,16,8,128]{3,2,1,0:T(8,128)(2,1)}, bf16[7,16,8,128]{3,2,1,0:T(8,128)(2,1)}, u32[]{:S(2)}, u32[]{:S(2)}) collective-permute-start(bf16[7,16,8,128]{3,2,1,0:T(8,128)(2,1)} %get-tuple-element.7), channel_id=1, source_target_pairs={{0,24},{8,0},{16,8},{24,16},{1,25},{9,1},{17,9},{25,17},{2,26},{10... | collective-permute-start | bytes 688136 | tf_op jit(solution)/shard_map/ppermute | solution.py:28
  10.5 0.0 collective-permute-start.3
  10.5 0.0 copy-done.1
  10.5 0.6 fusion.6
  11.2 1.1 collective-permute-done
  12.3 0.0 copy-start
  12.3 4.7 %collective-permute-done.1 = bf16[7,10,8,512]{3,2,1,0:T(8,128)(2,1)S(1)} collective-permute-done((bf16[7,10,8,512]{3,2,1,0:T(8,128)(2,1)S(1)}, bf16[7,10,8,512]{3,2,1,0:T(8,128)(2,1)S(1)}, u32[]{:S(2)}, u32[]{:S(2)}) %collective-permute-start.1) | collective-permute-done | bytes 573472 | tf_op jit(solution)/shard_map/ppermute | solution.py:22
  17.1 0.1 fusion.1
  17.2 2.2 %collective-permute-start.4 = (bf16[7,20,8,128]{3,2,1,0:T(8,128)(2,1)S(1)}, bf16[7,20,8,128]{3,2,1,0:T(8,128)(2,1)S(1)}, u32[]{:S(2)}, u32[]{:S(2)}) collective-permute-start(bf16[7,20,8,128]{3,2,1,0:T(8,128)(2,1)S(1)} %get-tuple-element.5), channel_id=1, source_target_pairs={{0,24},{8,0},{16,8},{24,16},{1,25},{9,1},{17,9},{25,17},{2,26},{10... | collective-permute-start | bytes 860168 | tf_op jit(solution)/shard_map/ppermute | solution.py:28
  19.4 0.7 multiply_divide_fusion
  20.1 0.0 copy-done
  20.1 0.3 copy.10
  21.0 0.1 pad_maximum_fusion.3.factor_ref
  21.1 0.0 collective-permute-start.2
  21.1 0.2 pad_maximum_fusion.ext_ref
  21.4 4.9 %collective-permute-done.4 = bf16[7,20,8,128]{3,2,1,0:T(8,128)(2,1)S(1)} collective-permute-done((bf16[7,20,8,128]{3,2,1,0:T(8,128)(2,1)S(1)}, bf16[7,20,8,128]{3,2,1,0:T(8,128)(2,1)S(1)}, u32[]{:S(2)}, u32[]{:S(2)}) %collective-permute-start.4) | collective-permute-done | bytes 286752 | tf_op jit(solution)/shard_map/ppermute | solution.py:28
  26.3 0.0 collective-permute-done.5
  26.3 1.0 pad_maximum_fusion.2.east_ref
  27.3 6.1 %collective-permute-done.2 = bf16[7,20,8,128]{3,2,1,0:T(8,128)(2,1)S(1)} collective-permute-done((bf16[7,20,8,128]{3,2,1,0:T(8,128)(2,1)S(1)}, bf16[7,20,8,128]{3,2,1,0:T(8,128)(2,1)S(1)}, u32[]{:S(2)}, u32[]{:S(2)}) %collective-permute-start.2) | collective-permute-done | bytes 286752 | tf_op jit(solution)/shard_map/ppermute | solution.py:28
  33.4 0.0 collective-permute-done.3
  33.4 1.0 pad_maximum_fusion.1.west_ref
  34.4 97.8 %shard_map.37 = bf16[7,16,8,512]{3,2,1,0:T(8,128)(2,1)S(1)} custom-call(f32[19]{0:T(128)S(1)} %pad_maximum_fusion.3.factor_ref, bf16[7,36,8,128]{3,2,1,0:T(8,128)(2,1)S(1)} %pad_maximum_fusion.1.west_ref, bf16[7,36,8,512]{3,2,1,0:T(8,128)(2,1)S(1)} %pad_maximum_fusion.ext_ref, bf16[7,36,8,128]{3,2,1,0:T(8,128)(2,1)S(1)} %pad_maximum_fusion.2.east_ref, ...), custom_call_target="tpu_custom_call" | custom-call | tf_op jit(solution)/shard_map/pallas_call | solution.py:245
  132.2 1.2 copy.6
  (5 shorter events, 0.1 us)
Async XLA Ops:
  1.7 8.8 %copy-start.1 = (s32[2,1,1]{0,2,1:T(1,128)S(1)}, s32[2,1,1]{0,2,1:T(1,128)}, u32[]{:S(2)}) copy-start(s32[2,1,1]{0,2,1:T(1,128)} %param.4) | copy-start | bytes 28
  1.8 10.4 %collective-permute-start = (bf16[7,10,8,512]{3,2,1,0:T(8,128)(2,1)S(1)}, bf16[7,10,8,512]{3,2,1,0:T(8,128)(2,1)S(1)}, u32[]{:S(2)}, u32[]{:S(2)}) collective-permute-start(bf16[7,10,8,512]{3,2,1,0:T(8,128)(2,1)S(1)} %get-tuple-element.10), channel_id=1, source_target_pairs={{0,1},{1,2},{2,3},{3,4},{4,5},{5,6},{6,7},{8,9},{9,10},{10,11},{11... | collective-permute-start | bytes 1720328 | tf_op jit(solution)/shard_map/ppermute | solution.py:22
  5.6 11.4 %collective-permute-start.1 = (bf16[7,10,8,512]{3,2,1,0:T(8,128)(2,1)S(1)}, bf16[7,10,8,512]{3,2,1,0:T(8,128)(2,1)S(1)}, u32[]{:S(2)}, u32[]{:S(2)}) collective-permute-start(bf16[7,10,8,512]{3,2,1,0:T(8,128)(2,1)S(1)} %get-tuple-element.9), channel_id=1, source_target_pairs={{1,0},{2,1},{3,2},{4,3},{5,4},{6,5},{7,6},{9,8},{10,9},{11,10},{12... | collective-permute-start | bytes 1720328 | tf_op jit(solution)/shard_map/ppermute | solution.py:22
  8.4 17.9 %collective-permute-start.5 = (bf16[7,16,8,128]{3,2,1,0:T(8,128)(2,1)}, bf16[7,16,8,128]{3,2,1,0:T(8,128)(2,1)}, u32[]{:S(2)}, u32[]{:S(2)}) collective-permute-start(bf16[7,16,8,128]{3,2,1,0:T(8,128)(2,1)} %get-tuple-element.7), channel_id=1, source_target_pairs={{0,24},{8,0},{16,8},{24,16},{1,25},{9,1},{17,9},{25,17},{2,26},{10... | collective-permute-start | bytes 688136 | tf_op jit(solution)/shard_map/ppermute | solution.py:28
  10.5 22.8 %collective-permute-start.3 = (bf16[7,16,8,128]{3,2,1,0:T(8,128)(2,1)S(1)}, bf16[7,16,8,128]{3,2,1,0:T(8,128)(2,1)}, u32[]{:S(2)}, u32[]{:S(2)}) collective-permute-start(bf16[7,16,8,128]{3,2,1,0:T(8,128)(2,1)S(1)} %get-tuple-element.8), channel_id=1, source_target_pairs={{0,8},{8,16},{16,24},{24,0},{1,9},{9,17},{17,25},{25,1},{2,10},{10... | collective-permute-start | bytes 688136 | tf_op jit(solution)/shard_map/ppermute | solution.py:28
  12.3 7.8 %copy-start = (s32[2,8,16,512]{3,2,1,0:T(8,128)S(1)}, s32[2,8,16,512]{3,2,1,0:T(8,128)}, u32[]{:S(2)}) copy-start(s32[2,8,16,512]{3,2,1,0:T(8,128)} %param.5) | copy-start | bytes 1572868
  17.2 9.0 %collective-permute-start.4 = (bf16[7,20,8,128]{3,2,1,0:T(8,128)(2,1)S(1)}, bf16[7,20,8,128]{3,2,1,0:T(8,128)(2,1)S(1)}, u32[]{:S(2)}, u32[]{:S(2)}) collective-permute-start(bf16[7,20,8,128]{3,2,1,0:T(8,128)(2,1)S(1)} %get-tuple-element.5), channel_id=1, source_target_pairs={{0,24},{8,0},{16,8},{24,16},{1,25},{9,1},{17,9},{25,17},{2,26},{10... | collective-permute-start | bytes 860168 | tf_op jit(solution)/shard_map/ppermute | solution.py:28
  21.1 12.2 %collective-permute-start.2 = (bf16[7,20,8,128]{3,2,1,0:T(8,128)(2,1)S(1)}, bf16[7,20,8,128]{3,2,1,0:T(8,128)(2,1)S(1)}, u32[]{:S(2)}, u32[]{:S(2)}) collective-permute-start(bf16[7,20,8,128]{3,2,1,0:T(8,128)(2,1)S(1)} %get-tuple-element.6), channel_id=1, source_target_pairs={{0,8},{8,16},{16,24},{24,0},{1,9},{9,17},{17,25},{25,1},{2,10},{10... | collective-permute-start | bytes 860168 | tf_op jit(solution)/shard_map/ppermute | solution.py:28

commit v5 on v4

--- a/solution.py
+++ b/solution.py
@@ -26,6 +26,17 @@
     count = lax.axis_size(axis)
     pairs = [(source, (source + steps) % count) for source in range(count)]
     return lax.ppermute(value, axis, pairs)
+
+
+def diagonal(value, lon_by, lat_by):
+    lons, lats = lax.axis_size("lon"), lax.axis_size("lat")
+    pairs = [
+        (i * lats + j, (i + lon_by) % lons * lats + j + lat_by)
+        for i in range(lons)
+        for j in range(lats)
+        if 0 <= j + lat_by < lats
+    ]
+    return lax.ppermute(value, ("lon", "lat"), pairs)
 
 
 def far(m):
@@ -218,12 +229,12 @@
     below = passed_along(fields[:, rows - HL :], "lat", 1)
     above = passed_along(fields[:, :HL], "lat", -1)
     tall = jnp.concatenate([below, fields, above], axis=1)
-    outer = jnp.concatenate([below, above], axis=1)
-
     def beside(lanes, steps):
-        own = from_behind(fields[..., lanes], "lon", steps)
-        halo = from_behind(outer[..., lanes], "lon", steps)
-        return jnp.concatenate([halo[:, :HL], own, halo[:, HL:]], axis=1)
+        edge = fields[..., lanes]
+        own = from_behind(edge, "lon", steps)
+        low = diagonal(edge[:, rows - HL :], steps, 1)
+        high = diagonal(edge[:, :HL], steps, -1)
+        return jnp.concatenate([low, own, high], axis=1)
 
     west = beside(slice(cols - LANES, cols), 1)
     east = beside(slice(0, LANES), -1)

time: 134 us -> 137 us (1.022)
  starting transfers between devices: 10.1 us -> 22.3 us
  waiting for transfers between devices: 16.8 us -> 6.83 us
  local copies, waits for them, and re-layouts: 5.01 us -> 6.68 us
    ppermute x0 -> x4, starting transfers between devices: none -> 14.1 us  [diagonal(): return lax.ppermute(value, ('lon', 'lat'), pairs)]
    ppermute x4 -> x2, waiting for transfers between devices: 10.9 us -> 4.98 us  [from_behind(): return lax.ppermute(value, axis, pairs)]
    ppermute x2, waiting for transfers between devices: 5.84 us -> 0.01 us  [passed_along(): return lax.ppermute(value, axis, pairs)]
    ppermute x4 -> x2, starting transfers between devices: 4.39 us -> 1.49 us  [from_behind(): return lax.ppermute(value, axis, pairs)]
    ppermute x0 -> x4, waiting for transfers between devices: none -> 1.84 us  [diagonal(): return lax.ppermute(value, ('lon', 'lat'), pairs)]
    unnamed x7 -> x4, local copies, waits for them, and re-layouts: 2.07 us -> 3.06 us
  transfers between devices with their start and end apart: 6 -> 8, of which waited for: 4 -> 2; matrix products, arithmetic and copies ran while one was open for 3% -> 3% of each run, Pallas kernels for 0% -> 0%
where the time goes in v5:
time: 137 us
  Pallas kernels  97.8 us (71%)
  starting transfers between devices  22.3 us (16%)
  waiting for transfers between devices  6.83 us (5%)
  local copies, waits for them, and re-layouts  6.68 us (5%)
  other arithmetic  2.14 us (2%)
    pallas_call x1, Pallas kernels, on_device(): pl.pallas_call(kernel, out_shape=jax.ShapeDtypeStruct((fields, rows, leve...  97.8 us
    ppermute x4, starting transfers between devices, diagonal(): return lax.ppermute(value, ('lon', 'lat'), pairs)  14.1 us
    ppermute x2, starting transfers between devices, passed_along(): return lax.ppermute(value, axis, pairs)  6.71 us
    ppermute x2, waiting for transfers between devices, from_behind(): return lax.ppermute(value, axis, pairs)  4.98 us
    unnamed x4, local copies, waits for them, and re-layouts  3.06 us
  transfers between devices with their start and end apart: 8, of which 2 were waited for; matrix products, arithmetic and copies ran while one was open for 3% of the time, Pallas kernels for 0%

profile of v5, /device:TPU:17, one launch (start us, length us, event | category | flops | bytes accessed | tf_op | source)
XLA Modules:
  0.0 136.6 jit_solution(15140754757427333612)
XLA Ops:
  0.0 1.7 %copy.9 = bf16[7,8,16,512]{3,1,2,0:T(8,128)(2,1)S(1)} copy(bf16[7,8,16,512]{3,2,1,0:T(8,128)(2,1)} %param.3) | data formatting | bytes 1835008 | tf_op args[0]
  1.7 0.0 copy-start
  1.7 0.9 fusion.1
  2.6 5.6 %collective-permute-start.5 = (bf16[7,10,8,128]{3,2,1,0:T(8,128)(2,1)}, bf16[7,10,8,128]{3,2,1,0:T(8,128)(2,1)}, u32[]{:S(2)}, u32[]{:S(2)}) collective-permute-start(bf16[7,10,8,128]{3,2,1,0:T(8,128)(2,1)} %get-tuple-element.5), channel_id=1, source_target_pairs={{0,25},{1,26},{2,27},{3,28},{4,29},{5,30},{6,31},{8,1},{9,2},{10,3... | collective-permute-start | bytes 430088 | tf_op jit(solution)/shard_map/ppermute | solution.py:39
  8.2 1.9 %collective-permute-start.7 = (bf16[7,10,8,128]{3,2,1,0:T(8,128)(2,1)}, bf16[7,10,8,128]{3,2,1,0:T(8,128)(2,1)}, u32[]{:S(2)}, u32[]{:S(2)}) collective-permute-start(bf16[7,10,8,128]{3,2,1,0:T(8,128)(2,1)} %get-tuple-element.6), channel_id=1, source_target_pairs={{1,24},{2,25},{3,26},{4,27},{5,28},{6,29},{7,30},{9,0},{10,1},{11,... | collective-permute-start | bytes 430088 | tf_op jit(solution)/shard_map/ppermute | solution.py:39
  10.2 0.8 fusion.2
  11.0 0.3 collective-permute-start.6
  11.2 0.1 fusion.3
  11.4 4.8 %collective-permute-start.3 = (bf16[7,10,8,512]{3,2,1,0:T(8,128)(2,1)S(1)}, bf16[7,10,8,512]{3,2,1,0:T(8,128)(2,1)S(1)}, u32[]{:S(2)}, u32[]{:S(2)}) collective-permute-start(bf16[7,10,8,512]{3,2,1,0:T(8,128)(2,1)S(1)} %get-tuple-element.11), channel_id=1, source_target_pairs={{0,1},{1,2},{2,3},{3,4},{4,5},{5,6},{6,7},{8,9},{9,10},{10,11},{11... | collective-permute-start | bytes 1720328 | tf_op jit(solution)/shard_map/ppermute | solution.py:22
  16.2 1.9 %collective-permute-start.4 = (bf16[7,10,8,512]{3,2,1,0:T(8,128)(2,1)S(1)}, bf16[7,10,8,512]{3,2,1,0:T(8,128)(2,1)S(1)}, u32[]{:S(2)}, u32[]{:S(2)}) collective-permute-start(bf16[7,10,8,512]{3,2,1,0:T(8,128)(2,1)S(1)} %get-tuple-element.12), channel_id=1, source_target_pairs={{1,0},{2,1},{3,2},{4,3},{5,4},{6,5},{7,6},{9,8},{10,9},{11,10},{12... | collective-permute-start | bytes 1720328 | tf_op jit(solution)/shard_map/ppermute | solution.py:22
  18.1 0.0 copy-done
  18.1 0.6 fusion.4
  19.4 0.6 multiply_divide_fusion
  20.0 0.0 collective-permute-done.5
  20.0 3.7 %collective-permute-start = (bf16[7,10,8,128]{3,2,1,0:T(8,128)(2,1)}, bf16[7,10,8,128]{3,2,1,0:T(8,128)(2,1)S(1)}, u32[]{:S(2)}, u32[]{:S(2)}) collective-permute-start(bf16[7,10,8,128]{3,2,1,0:T(8,128)(2,1)} %get-tuple-element.8), channel_id=1, source_target_pairs={{0,9},{1,10},{2,11},{3,12},{4,13},{5,14},{6,15},{8,17},{9,18},{10,... | collective-permute-start | bytes 430088 | tf_op jit(solution)/shard_map/ppermute | solution.py:39
  23.7 0.0 collective-permute-done.7
  23.7 2.8 %collective-permute-start.2 = (bf16[7,10,8,128]{3,2,1,0:T(8,128)(2,1)}, bf16[7,10,8,128]{3,2,1,0:T(8,128)(2,1)S(1)}, u32[]{:S(2)}, u32[]{:S(2)}) collective-permute-start(bf16[7,10,8,128]{3,2,1,0:T(8,128)(2,1)} %get-tuple-element.7), channel_id=1, source_target_pairs={{1,8},{2,9},{3,10},{4,11},{5,12},{6,13},{7,14},{9,16},{10,17},{11,... | collective-permute-start | bytes 430088 | tf_op jit(solution)/shard_map/ppermute | solution.py:39
  26.6 0.0 collective-permute-done.6
  26.6 1.2 collective-permute-start.1
  27.8 0.1 pad_maximum_fusion.3.factor_ref
  27.9 1.4 copy.10
  29.2 1.2 pad_maximum_fusion.2.east_ref
  30.4 0.0 collective-permute-done
  30.4 1.8 %collective-permute-done.2 = bf16[7,10,8,128]{3,2,1,0:T(8,128)(2,1)S(1)} collective-permute-done((bf16[7,10,8,128]{3,2,1,0:T(8,128)(2,1)}, bf16[7,10,8,128]{3,2,1,0:T(8,128)(2,1)S(1)}, u32[]{:S(2)}, u32[]{:S(2)}) %collective-permute-start.2) | collective-permute-done | bytes 143392 | tf_op jit(solution)/shard_map/ppermute | solution.py:39
  32.2 5.0 %collective-permute-done.1 = bf16[7,16,8,128]{3,2,1,0:T(8,128)(2,1)S(1)} collective-permute-done((bf16[7,16,8,128]{3,2,1,0:T(8,128)(2,1)S(1)}, bf16[7,16,8,128]{3,2,1,0:T(8,128)(2,1)S(1)}, u32[]{:S(2)}, u32[]{:S(2)}) %collective-permute-start.1) | collective-permute-done | bytes 229408 | tf_op jit(solution)/shard_map/ppermute | solution.py:28
  37.2 0.1 pad_maximum_fusion.1.west_ref
  37.3 0.0 collective-permute-done.3
  37.3 0.0 collective-permute-done.4
  37.3 0.2 pad_maximum_fusion.ext_ref
  37.5 97.8 %shard_map.37 = bf16[7,16,8,512]{3,2,1,0:T(8,128)(2,1)S(1)} custom-call(f32[19]{0:T(128)S(1)} %pad_maximum_fusion.3.factor_ref, bf16[7,36,8,128]{3,2,1,0:T(8,128)(2,1)S(1)} %pad_maximum_fusion.1.west_ref, bf16[7,36,8,512]{3,2,1,0:T(8,128)(2,1)S(1)} %pad_maximum_fusion.ext_ref, bf16[7,36,8,128]{3,2,1,0:T(8,128)(2,1)S(1)} %pad_maximum_fusion.2.east_ref, ...), custom_call_target="tpu_custom_call" | custom-call | tf_op jit(solution)/shard_map/pallas_call | solution.py:256
  135.3 1.2 copy.6
  (1 shorter events, 0.0 us)
Async XLA Ops:
  1.7 16.4 %copy-start = (s32[2,1,1]{0,2,1:T(1,128)S(1)}, s32[2,1,1]{0,2,1:T(1,128)}, u32[]{:S(2)}) copy-start(s32[2,1,1]{0,2,1:T(1,128)} %param.4) | copy-start | bytes 28
  2.6 17.4 %collective-permute-start.5 = (bf16[7,10,8,128]{3,2,1,0:T(8,128)(2,1)}, bf16[7,10,8,128]{3,2,1,0:T(8,128)(2,1)}, u32[]{:S(2)}, u32[]{:S(2)}) collective-permute-start(bf16[7,10,8,128]{3,2,1,0:T(8,128)(2,1)} %get-tuple-element.5), channel_id=1, source_target_pairs={{0,25},{1,26},{2,27},{3,28},{4,29},{5,30},{6,31},{8,1},{9,2},{10,3... | collective-permute-start | bytes 430088 | tf_op jit(solution)/shard_map/ppermute | solution.py:39
  8.2 15.4 %collective-permute-start.7 = (bf16[7,10,8,128]{3,2,1,0:T(8,128)(2,1)}, bf16[7,10,8,128]{3,2,1,0:T(8,128)(2,1)}, u32[]{:S(2)}, u32[]{:S(2)}) collective-permute-start(bf16[7,10,8,128]{3,2,1,0:T(8,128)(2,1)} %get-tuple-element.6), channel_id=1, source_target_pairs={{1,24},{2,25},{3,26},{4,27},{5,28},{6,29},{7,30},{9,0},{10,1},{11,... | collective-permute-start | bytes 430088 | tf_op jit(solution)/shard_map/ppermute | solution.py:39
  11.0 15.6 %collective-permute-start.6 = (bf16[7,16,8,128]{3,2,1,0:T(8,128)(2,1)}, bf16[7,16,8,128]{3,2,1,0:T(8,128)(2,1)}, u32[]{:S(2)}, u32[]{:S(2)}) collective-permute-start(bf16[7,16,8,128]{3,2,1,0:T(8,128)(2,1)} %get-tuple-element.9), channel_id=1, source_target_pairs={{0,24},{8,0},{16,8},{24,16},{1,25},{9,1},{17,9},{25,17},{2,26},{10... | collective-permute-start | bytes 688136 | tf_op jit(solution)/shard_map/ppermute | solution.py:28
  11.4 25.9 %collective-permute-start.3 = (bf16[7,10,8,512]{3,2,1,0:T(8,128)(2,1)S(1)}, bf16[7,10,8,512]{3,2,1,0:T(8,128)(2,1)S(1)}, u32[]{:S(2)}, u32[]{:S(2)}) collective-permute-start(bf16[7,10,8,512]{3,2,1,0:T(8,128)(2,1)S(1)} %get-tuple-element.11), channel_id=1, source_target_pairs={{0,1},{1,2},{2,3},{3,4},{4,5},{5,6},{6,7},{8,9},{9,10},{10,11},{11... | collective-permute-start | bytes 1720328 | tf_op jit(solution)/shard_map/ppermute | solution.py:22
  16.2 21.1 %collective-permute-start.4 = (bf16[7,10,8,512]{3,2,1,0:T(8,128)(2,1)S(1)}, bf16[7,10,8,512]{3,2,1,0:T(8,128)(2,1)S(1)}, u32[]{:S(2)}, u32[]{:S(2)}) collective-permute-start(bf16[7,10,8,512]{3,2,1,0:T(8,128)(2,1)S(1)} %get-tuple-element.12), channel_id=1, source_target_pairs={{1,0},{2,1},{3,2},{4,3},{5,4},{6,5},{7,6},{9,8},{10,9},{11,10},{12... | collective-permute-start | bytes 1720328 | tf_op jit(solution)/shard_map/ppermute | solution.py:22
  20.0 10.4 %collective-permute-start = (bf16[7,10,8,128]{3,2,1,0:T(8,128)(2,1)}, bf16[7,10,8,128]{3,2,1,0:T(8,128)(2,1)S(1)}, u32[]{:S(2)}, u32[]{:S(2)}) collective-permute-start(bf16[7,10,8,128]{3,2,1,0:T(8,128)(2,1)} %get-tuple-element.8), channel_id=1, source_target_pairs={{0,9},{1,10},{2,11},{3,12},{4,13},{5,14},{6,15},{8,17},{9,18},{10,... | collective-permute-start | bytes 430088 | tf_op jit(solution)/shard_map/ppermute | solution.py:39
  23.7 8.5 %collective-permute-start.2 = (bf16[7,10,8,128]{3,2,1,0:T(8,128)(2,1)}, bf16[7,10,8,128]{3,2,1,0:T(8,128)(2,1)S(1)}, u32[]{:S(2)}, u32[]{:S(2)}) collective-permute-start(bf16[7,10,8,128]{3,2,1,0:T(8,128)(2,1)} %get-tuple-element.7), channel_id=1, source_target_pairs={{1,8},{2,9},{3,10},{4,11},{5,12},{6,13},{7,14},{9,16},{10,17},{11,... | collective-permute-start | bytes 430088 | tf_op jit(solution)/shard_map/ppermute | solution.py:39
  26.6 10.6 %collective-permute-start.1 = (bf16[7,16,8,128]{3,2,1,0:T(8,128)(2,1)S(1)}, bf16[7,16,8,128]{3,2,1,0:T(8,128)(2,1)S(1)}, u32[]{:S(2)}, u32[]{:S(2)}) collective-permute-start(bf16[7,16,8,128]{3,2,1,0:T(8,128)(2,1)S(1)} %get-tuple-element.10), channel_id=1, source_target_pairs={{0,8},{8,16},{16,24},{24,0},{1,9},{9,17},{17,25},{25,1},{2,10},{10... | collective-permute-start | bytes 688136 | tf_op jit(solution)/shard_map/ppermute | solution.py:28
